TPU v7x, 256 devices: a whole 4x4x8 slice. The times are simulated.
256 devices in a mesh: ctx: 16 (over z_hi, y, core), dp: 16 (over x, z_lo).
Axes of the slice: x: 4, y: 4, z: 8 (z_hi: 2, z_lo: 4; z = z_hi * 4 + z_lo), core: 2. Of those that a mesh axis runs over, the one named last changes fastest.
Arguments:
- queries: bfloat16 [16, 2048, 4096], P('dp', 'ctx'), may hold values from -180 to 180
- keys: bfloat16 [16, 2048, 512], P('dp', 'ctx'), may hold values from -18 to 18
- values: bfloat16 [16, 2048, 512], P('dp', 'ctx'), may hold values from -6 to 6
- grad_out: bfloat16 [16, 2048, 4096], P('dp', 'ctx'), may hold values from -6 to 6
- doc_lengths: int32 [16, 16], P('dp'), may hold values from 1 to 256, 2048 in all within a row
- placement: int32 [16, 16, 16], P('dp'), may hold values from 0 to 15, each once within a row
Outputs:
- attn_out: bfloat16 [16, 2048, 4096], P('dp', 'ctx')
- grad_q: bfloat16 [16, 2048, 4096], P('dp', 'ctx')
- grad_k: bfloat16 [16, 2048, 512], P('dp', 'ctx')
- grad_v: bfloat16 [16, 2048, 512], P('dp', 'ctx')
- grad_bias: float32 [5120], replicated
Inputs may be any that keep to these rules, and one draw needn't show every extreme that they name: `doc_lengths`: each row sums to 2048, and its longest document has exactly 256 rows. placement[b, s, j] is the device that works on block j (rows j * 8 to j * 8 + 7) of device s's 128 rows; each placement[b, s] is a permutation of 0 to 15.
All inputs are finite; a program needn't handle non-finite values.
Results may differ from a plain program's by a relative error of at most 0.0095.
Values may be sent and summed in bfloat16 or wider, within the bound.
A program may use at most 128 MiB of HBM per device.

v0:
```python
import math

import jax
import jax.numpy as jnp
from jax import lax
from jax.sharding import PartitionSpec as P

HD = 128
HQ = 32
HK = 4
DOC_MOST = 256


def doc_index(starts, positions):
    return jnp.sum((starts[None, :] <= positions[:, None]).astype(jnp.int32), axis=1) - 1


def block_attention(
    query_block, dout_block, key_window, value_window, query_pos, query_doc, key_pos, key_doc
):
    row_count = query_block.shape[0]
    key_count = key_window.shape[0]
    group_size = HQ // HK
    score_scale = 1.0 / math.sqrt(HD)
    query_heads = query_block.reshape(row_count, HK, group_size, HD)
    dout_heads = dout_block.reshape(row_count, HK, group_size, HD)
    key_heads = key_window.reshape(key_count, HK, HD)
    value_heads = value_window.reshape(key_count, HK, HD)
    scores = (
        jnp.einsum("rgnd,wgd->gnrw", query_heads, key_heads, preferred_element_type=jnp.float32)
        * score_scale
    )
    allowed = (query_doc[:, None] == key_doc[None, :]) & (key_pos[None, :] <= query_pos[:, None])
    scores = jnp.where(allowed, scores, -1e30)
    row_top = jnp.max(scores, axis=-1, keepdims=True)
    exponents = jnp.where(allowed, jnp.exp(scores - row_top), 0.0)
    probs = exponents / jnp.sum(exponents, axis=-1, keepdims=True)
    weights = probs.astype(jnp.bfloat16)
    context = jnp.einsum("gnrw,wgd->rgnd", weights, value_heads, preferred_element_type=jnp.float32)
    delta_sum = jnp.sum(dout_heads.astype(jnp.float32) * context, axis=3)
    prob_grad = jnp.einsum(
        "rgnd,wgd->gnrw", dout_heads, value_heads, preferred_element_type=jnp.float32
    )
    score_grad = (
        probs * (prob_grad - jnp.transpose(delta_sum, (1, 2, 0))[..., None]) * score_scale
    ).astype(jnp.bfloat16)
    query_grad = jnp.einsum(
        "gnrw,wgd->rgnd", score_grad, key_heads, preferred_element_type=jnp.float32
    ).reshape(row_count, -1)
    key_grad = jnp.einsum(
        "gnrw,rgnd->wgd", score_grad, query_heads, preferred_element_type=jnp.float32
    ).reshape(key_count, -1)
    value_grad = jnp.einsum(
        "gnrw,rgnd->wgd", weights, dout_heads, preferred_element_type=jnp.float32
    ).reshape(key_count, -1)
    return (context.reshape(row_count, -1), query_grad, key_grad, value_grad)


def run_blocks(
    query_blocks, dout_blocks, block_starts, key_bank, value_bank, bank_base, starts, width, groups
):
    block_count, block_rows = (query_blocks.shape[0], query_blocks.shape[1])
    per_group = block_count // groups
    bank_rows = key_bank.shape[0]
    key_cols = key_bank.shape[1]
    empty_terms = jnp.zeros((bank_rows, key_cols), jnp.float32)
    window_iota = jnp.arange(width, dtype=jnp.int32)

    def one_block(query_block, dout_block, block_start):
        query_pos = block_start + jnp.arange(block_rows, dtype=jnp.int32)
        window_start = jnp.clip(block_start + block_rows - width - bank_base, 0, bank_rows - width)
        key_window = lax.dynamic_slice_in_dim(key_bank, window_start, width, 0)
        value_window = lax.dynamic_slice_in_dim(value_bank, window_start, width, 0)
        key_pos = bank_base + window_start + window_iota
        context, query_grad, key_grad, value_grad = block_attention(
            query_block,
            dout_block,
            key_window,
            value_window,
            query_pos,
            doc_index(starts, query_pos),
            key_pos,
            doc_index(starts, key_pos),
        )
        return (context, query_grad, key_grad, value_grad, window_start)

    def group_step(totals, inputs):
        query_group, dout_group, start_group = inputs
        context, query_grad, key_grad, value_grad, window_start = jax.vmap(one_block)(
            query_group, dout_group, start_group
        )
        rows_hit = (window_start[:, None] + window_iota[None, :]).reshape(-1)
        key_total = totals[0].at[rows_hit].add(key_grad.reshape(-1, key_cols))
        value_total = totals[1].at[rows_hit].add(value_grad.reshape(-1, key_cols))
        return ((key_total, value_total), (context, query_grad))

    grouped = (
        query_blocks.reshape(groups, per_group, block_rows, -1),
        dout_blocks.reshape(groups, per_group, block_rows, -1),
        block_starts.reshape(groups, per_group),
    )
    totals, outputs = lax.scan(group_step, (empty_terms, empty_terms), grouped)
    contexts, query_grads = outputs
    return (
        totals,
        (
            contexts.reshape(block_count, block_rows, -1),
            query_grads.reshape(block_count, block_rows, -1),
        ),
    )


def local(queries, keys, values, grad_out, doc_lengths, placement):
    query_rows = queries[0]
    key_rows = keys[0]
    value_rows = values[0]
    dout_rows = grad_out[0]
    lengths = doc_lengths[0]
    layout = placement[0]
    ctx_count = lax.axis_size("ctx")
    device = lax.axis_index("ctx")
    shard_rows = query_rows.shape[0]
    block_rows = shard_rows // ctx_count
    starts = jnp.cumsum(lengths) - lengths
    devices_iota = jnp.arange(ctx_count, dtype=jnp.int32)
    source_block = jnp.sum(
        jnp.where(
            layout[:, :, None] == devices_iota[None, None, :], devices_iota[None, :, None], 0
        ),
        axis=1,
    )
    send_order = source_block[device]
    query_blocks = query_rows.reshape(ctx_count, block_rows, -1)
    dout_blocks = dout_rows.reshape(ctx_count, block_rows, -1)
    send_query = jnp.take(query_blocks, send_order, axis=0)
    send_dout = jnp.take(dout_blocks, send_order, axis=0)
    placed_query, placed_dout = (
        lax.all_to_all(send_query, "ctx", split_axis=0, concat_axis=0, tiled=True),
        lax.all_to_all(send_dout, "ctx", split_axis=0, concat_axis=0, tiled=True),
    )
    block_starts = devices_iota * shard_rows + source_block[:, device] * block_rows
    all_keys, all_values = (
        lax.all_gather(key_rows, "ctx", axis=0, tiled=True),
        lax.all_gather(value_rows, "ctx", axis=0, tiled=True),
    )
    groups = 2
    totals, outputs = run_blocks(
        placed_query,
        placed_dout,
        block_starts,
        all_keys,
        all_values,
        0,
        starts,
        DOC_MOST + block_rows,
        groups,
    )
    contexts, query_grads = outputs
    key_grad, value_grad = (
        lax.psum_scatter(totals[0], "ctx", scatter_dimension=0, tiled=True),
        lax.psum_scatter(totals[1], "ctx", scatter_dimension=0, tiled=True),
    )
    attn_rows = contexts.reshape(shard_rows, -1).astype(jnp.bfloat16)
    query_grad_rows = query_grads.reshape(shard_rows, -1).astype(jnp.bfloat16)
    bias_parts = lax.psum(
        (jnp.sum(query_grads, axis=(0, 1)), jnp.sum(key_grad, axis=0), jnp.sum(value_grad, axis=0)),
        ("ctx", "dp"),
    )
    grad_bias = jnp.concatenate(bias_parts)
    return (
        attn_rows[None],
        query_grad_rows[None],
        key_grad.astype(jnp.bfloat16)[None],
        value_grad.astype(jnp.bfloat16)[None],
        grad_bias,
    )


def solution(mesh):
    return jax.shard_map(
        local,
        mesh=mesh,
        in_specs=(
            P("dp", "ctx", None),
            P("dp", "ctx", None),
            P("dp", "ctx", None),
            P("dp", "ctx", None),
            P("dp", None),
            P("dp", None, None),
        ),
        out_specs=(
            P("dp", "ctx", None),
            P("dp", "ctx", None),
            P("dp", "ctx", None),
            P("dp", "ctx", None),
            P(),
        ),
        check_vma=False,
    )
```

profile of v0, /device:TPU:1, one launch (start us, length us, event | category | flops | bytes accessed | tf_op | source)
XLA Modules:
  0.0 738.5 jit_solution(11102240974573667914)
XLA Ops:
  9.4 1.8 gather_fusion.1
  12.8 12.7 %all-to-all-start = ((bf16[16,8,4096]{2,1,0:T(8,128)(2,1)}), bf16[16,8,4096]{2,1,0:T(8,128)(2,1)S(1)}, u32[]{:S(2)}, u32[]{:S(2)}) async-start(bf16[16,8,4096]{2,1,0:T(8,128)(2,1)} %get-tuple-element.386), calls=%async_computation | async-start | bytes 2097152 | tf_op jit(solution)/shard_map/all_to_all | solution.py:138
  26.3 23.8 %all-to-all-done = bf16[16,8,4096]{2,1,0:T(8,128)(2,1)S(1)} async-done(((bf16[16,8,4096]{2,1,0:T(8,128)(2,1)}), bf16[16,8,4096]{2,1,0:T(8,128)(2,1)S(1)}, u32[]{:S(2)}, u32[]{:S(2)}) %all-to-all-start) | async-done | bytes 1048608 | tf_op jit(solution)/shard_map/all_to_all | solution.py:138
  50.1 9.5 %all-to-all-start.1 = ((bf16[16,8,4096]{2,1,0:T(8,128)(2,1)}), bf16[16,8,4096]{2,1,0:T(8,128)(2,1)S(1)}, u32[]{:S(2)}, u32[]{:S(2)}) async-start(bf16[16,8,4096]{2,1,0:T(8,128)(2,1)} %get-tuple-element.385), calls=%async_computation.1 | async-start | bytes 2097152 | tf_op jit(solution)/shard_map/all_to_all | solution.py:139
  60.2 25.8 %all-to-all-done.1 = bf16[16,8,4096]{2,1,0:T(8,128)(2,1)S(1)} async-done(((bf16[16,8,4096]{2,1,0:T(8,128)(2,1)}), bf16[16,8,4096]{2,1,0:T(8,128)(2,1)S(1)}, u32[]{:S(2)}, u32[]{:S(2)}) %all-to-all-start.1) | async-done | bytes 1048608 | tf_op jit(solution)/shard_map/all_to_all | solution.py:139
  86.0 3.0 all-gather.5.cloned.1.call-done
  89.1 77.6 %all-gather.7.cloned.1.call-done = bf16[1,2048,512]{2,1,0:T(8,128)(2,1)} async-done(((bf16[1,128,512]{2,1,0:T(8,128)(2,1)}), bf16[1,2048,512]{2,1,0:T(8,128)(2,1)}) %all-gather.7.cloned.1.call-update) | async-done | bytes 2097168 | tf_op jit(solution)/shard_map/all_gather | solution.py:144
  166.7 2.5 broadcast_in_dim.109
  169.2 2.5 broadcast_in_dim.109.clone
  171.6 279.6 %while.30 = (s32[]{:T(128)}, f32[2048,512]{1,0:T(8,128)}, f32[2048,512]{1,0:T(8,128)}, bf16[2,8,8,4096]{3,2,1,0:T(8,128)(2,1)}, f32[2,8,8,4096]{3,2,1,0:T(8,128)...) while((s32[]{:T(128)}, f32[2048,512]{1,0:T(8,128)}, ...), condition=%wide.region_10.12_spmd.clone, body=%wide.region_2.11_spmd.clone.sunk | while | flops 841414784 | bytes 167731056 | solution.py:102
  173.1 18.4 %while.32 = (s32[]{:T(128)}, bf16[2048,512]{1,0:T(8,128)(2,1)}, s32[8,2]{0,1:T(2,128)S(1)}, bf16[8,264,512]{2,1,0:T(8,128)(2,1)S(1)}, s32[]{:T(128)}) while((s32[]{:T(128)}, bf16[2048,512]{1,0:T(8,128)(2,1)}, s32[8,2]{0,1:T(2,128)S(1)}, bf16[8,264,512]{2,1,0:T(8,128)(2,1)S(1)}, s32[]{:T(128)}) %tuple.98), condition=%wide.while_cond, body=%wide.while_body.sunk | while | flops 2 | bytes 540769 | solution.py:72
  173.7 1.7 bitcast_dynamic-update-slice_fusion.5
  178.3 1.7 bitcast_dynamic-update-slice_fusion.5
  182.9 1.7 bitcast_dynamic-update-slice_fusion.5
  185.2 1.7 bitcast_dynamic-update-slice_fusion.5
  187.5 1.7 bitcast_dynamic-update-slice_fusion.5
  189.8 1.7 bitcast_dynamic-update-slice_fusion.5
  192.8 3.9 reshape.437
  199.7 11.5 %fusion.80 = (f32[8,4,8,8]{2,3,1,0:T(8,128)S(1)}, f32[8,4,8,8,264]{4,2,3,1,0:T(8,128)S(1)}) fusion(f32[8,4,264,8,8]{2,4,3,1,0:T(8,128)S(1)} %fusion.79, pred[8,8,264]{2,1,0:T(8,128)(4,1)S(1)} %compare_and_fusion.3), kind=kOutput, calls=%fused_computation.80.clone.1 | output fusion | flops 3784967 | bytes 4350464 | tf_op jit(solution)/shard_map/while/body/eval_jaxpr/vmap()/sub | solution.py:36
  211.2 1.8 fusion.81
  214.5 23.8 %while.31 = (s32[]{:T(128)}, bf16[2048,512]{1,0:T(8,128)(2,1)}, s32[8,2]{0,1:T(2,128)S(1)}, bf16[8,264,512]{2,1,0:T(8,128)(2,1)}, s32[]{:T(128)}) while((s32[]{:T(128)}, bf16[2048,512]{1,0:T(8,128)(2,1)}, s32[8,2]{0,1:T(2,128)S(1)}, bf16[8,264,512]{2,1,0:T(8,128)(2,1)}, s32[]{:T(128)}) %tuple.116), condition=%wide.while_cond.1, body=%wide.while_body.1.sunk | while | flops 2 | bytes 541785 | solution.py:73
  215.1 2.4 bitcast_dynamic-update-slice_fusion.4
  218.0 2.4 bitcast_dynamic-update-slice_fusion.4
  221.0 2.4 bitcast_dynamic-update-slice_fusion.4
  224.0 2.4 bitcast_dynamic-update-slice_fusion.4
  226.9 2.4 bitcast_dynamic-update-slice_fusion.4
  229.9 2.4 bitcast_dynamic-update-slice_fusion.4
  232.9 2.4 bitcast_dynamic-update-slice_fusion.4
  235.9 2.4 bitcast_dynamic-update-slice_fusion.4
  238.3 4.8 reshape.436
  244.1 4.2 fusion.82
  250.5 4.3 fusion.84
  260.0 3.2 copy.167
  263.3 21.8 %scatter_custom_fusion.12 = f32[2048,512]{1,0:T(8,128)} fusion(f32[2048,512]{1,0:T(8,128)} %get-tuple-element.590, s32[2112]{0:T(1024)S(1)} %fusion.78, f32[264,8,4,128]{3,2,1,0:T(4,128)} %bitcast.165), kind=kCustom, calls=%fused_computation.13.clone.1 | custom fusion | flops 1081344 | bytes 8519680 | tf_op jit(solution)/shard_map/while/body/eval_jaxpr/scatter-add | solution.py:93
  286.5 3.1 copy.168
  289.6 21.8 %scatter_custom_fusion.13 = f32[2048,512]{1,0:T(8,128)} fusion(f32[2048,512]{1,0:T(8,128)} %get-tuple-element.591, s32[2112]{0:T(1024)S(1)} %fusion.78, f32[264,8,4,128]{3,2,1,0:T(4,128)} %bitcast.166), kind=kCustom, calls=%fused_computation.10.clone.1 | custom fusion | flops 1081344 | bytes 8519680 | tf_op jit(solution)/shard_map/while/body/eval_jaxpr/scatter-add | solution.py:94
  312.9 18.4 %while.32 = (s32[]{:T(128)}, bf16[2048,512]{1,0:T(8,128)(2,1)}, s32[8,2]{0,1:T(2,128)S(1)}, bf16[8,264,512]{2,1,0:T(8,128)(2,1)S(1)}, s32[]{:T(128)}) while((s32[]{:T(128)}, bf16[2048,512]{1,0:T(8,128)(2,1)}, s32[8,2]{0,1:T(2,128)S(1)}, bf16[8,264,512]{2,1,0:T(8,128)(2,1)S(1)}, s32[]{:T(128)}) %tuple.98), condition=%wide.while_cond, body=%wide.while_body.sunk | while | flops 2 | bytes 540769 | solution.py:72
  315.8 1.7 bitcast_dynamic-update-slice_fusion.5
  320.4 1.7 bitcast_dynamic-update-slice_fusion.5
  325.0 1.7 bitcast_dynamic-update-slice_fusion.5
  332.6 3.9 reshape.437
  339.5 11.5 %fusion.80 = (f32[8,4,8,8]{2,3,1,0:T(8,128)S(1)}, f32[8,4,8,8,264]{4,2,3,1,0:T(8,128)S(1)}) fusion(f32[8,4,264,8,8]{2,4,3,1,0:T(8,128)S(1)} %fusion.79, pred[8,8,264]{2,1,0:T(8,128)(4,1)S(1)} %compare_and_fusion.3), kind=kOutput, calls=%fused_computation.80.clone.1 | output fusion | flops 3784967 | bytes 4350464 | tf_op jit(solution)/shard_map/while/body/eval_jaxpr/vmap()/sub | solution.py:36
  351.0 1.8 fusion.81
  354.3 23.8 %while.31 = (s32[]{:T(128)}, bf16[2048,512]{1,0:T(8,128)(2,1)}, s32[8,2]{0,1:T(2,128)S(1)}, bf16[8,264,512]{2,1,0:T(8,128)(2,1)}, s32[]{:T(128)}) while((s32[]{:T(128)}, bf16[2048,512]{1,0:T(8,128)(2,1)}, s32[8,2]{0,1:T(2,128)S(1)}, bf16[8,264,512]{2,1,0:T(8,128)(2,1)}, s32[]{:T(128)}) %tuple.116), condition=%wide.while_cond.1, body=%wide.while_body.1.sunk | while | flops 2 | bytes 541785 | solution.py:73
  354.9 2.4 bitcast_dynamic-update-slice_fusion.4
  357.9 2.4 bitcast_dynamic-update-slice_fusion.4
  360.8 2.4 bitcast_dynamic-update-slice_fusion.4
  363.8 2.4 bitcast_dynamic-update-slice_fusion.4
  366.7 2.4 bitcast_dynamic-update-slice_fusion.4
  369.7 2.4 bitcast_dynamic-update-slice_fusion.4
  372.7 2.4 bitcast_dynamic-update-slice_fusion.4
  375.7 2.4 bitcast_dynamic-update-slice_fusion.4
  378.1 4.8 reshape.436
  383.9 4.2 fusion.82
  390.3 4.3 fusion.84
  399.8 3.2 copy.167
  403.1 21.8 %scatter_custom_fusion.12 = f32[2048,512]{1,0:T(8,128)} fusion(f32[2048,512]{1,0:T(8,128)} %get-tuple-element.590, s32[2112]{0:T(1024)S(1)} %fusion.78, f32[264,8,4,128]{3,2,1,0:T(4,128)} %bitcast.165), kind=kCustom, calls=%fused_computation.13.clone.1 | custom fusion | flops 1081344 | bytes 8519680 | tf_op jit(solution)/shard_map/while/body/eval_jaxpr/scatter-add | solution.py:93
  426.3 3.1 copy.168
  429.4 21.8 %scatter_custom_fusion.13 = f32[2048,512]{1,0:T(8,128)} fusion(f32[2048,512]{1,0:T(8,128)} %get-tuple-element.591, s32[2112]{0:T(1024)S(1)} %fusion.78, f32[264,8,4,128]{3,2,1,0:T(4,128)} %bitcast.166), kind=kCustom, calls=%fused_computation.10.clone.1 | custom fusion | flops 1081344 | bytes 8519680 | tf_op jit(solution)/shard_map/while/body/eval_jaxpr/scatter-add | solution.py:94
  454.0 95.5 %reduce-scatter.3.cloned.1.call-done = f32[128,512]{1,0:T(8,128)} async-done(((f32[2048,512]{1,0:T(8,128)}), f32[128,512]{1,0:T(8,128)}) %reduce-scatter.3.cloned.1.call-update) | async-done | bytes 262160 | tf_op jit(solution)/shard_map/reduce_scatter | solution.py:160
  549.5 1.8 fusion.41
  551.2 103.0 %reduce-scatter.5.cloned.1.call-done = f32[128,512]{1,0:T(8,128)} async-done(((f32[2048,512]{1,0:T(8,128)}), f32[128,512]{1,0:T(8,128)}) %reduce-scatter.5.cloned.1.call-update) | async-done | bytes 262160 | tf_op jit(solution)/shard_map/reduce_scatter | solution.py:161
  654.3 1.7 fusion.42
  656.0 75.4 %all-reduce.1 = (f32[512]{0:T(512)S(1)}, f32[512]{0:T(512)S(1)}, f32[4096]{0:T(1024)S(1)}) all-reduce(f32[512]{0:T(512)S(1)} %get-tuple-element.383, f32[512]{0:T(512)S(1)} %get-tuple-element.381, f32[4096]{0:T(1024)S(1)} %get-tuple-element.379), channel_id=1, replica_groups=mesh['ctx'=16,'dp'=16] {'ctx','dp'}, use_global_device_ids=true, to_apply=%region_18.20 | all-reduce | flops 5120 | bytes 40960 | tf_op jit(solution)/shard_map/psum | solution.py:165
  (211 shorter events, 73.0 us)
Async XLA Ops:
  7.2 1.6 copy-start
  7.2 81.9 %all-gather.5.cloned.1.call-start = ((), (), s32[]{:S(2)}) async-start(), calls=%async_computation.6 | async-start | bytes 2228224 | tf_op jit(solution)/shard_map/all_gather | solution.py:143
  12.8 47.2 %copy-start.16 = (s32[1,16]{1,0:T(1,128)S(1)}, s32[1,16]{1,0:T(1,128)}, u32[]{:S(2)}) copy-start(s32[1,16]{1,0:T(1,128)} %param.14) | copy-start | bytes 196
  12.8 37.3 %all-to-all-start = ((bf16[16,8,4096]{2,1,0:T(8,128)(2,1)}), bf16[16,8,4096]{2,1,0:T(8,128)(2,1)S(1)}, u32[]{:S(2)}, u32[]{:S(2)}) async-start(bf16[16,8,4096]{2,1,0:T(8,128)(2,1)} %get-tuple-element.386), calls=%async_computation | async-start | bytes 2097152 | tf_op jit(solution)/shard_map/all_to_all | solution.py:138
  25.6 141.1 %all-gather.7.cloned.1.call-start = ((), (), s32[]{:S(2)}) async-start(), calls=%async_computation.7 | async-start | bytes 2228224 | tf_op jit(solution)/shard_map/all_gather | solution.py:144
  50.1 35.9 %all-to-all-start.1 = ((bf16[16,8,4096]{2,1,0:T(8,128)(2,1)}), bf16[16,8,4096]{2,1,0:T(8,128)(2,1)S(1)}, u32[]{:S(2)}, u32[]{:S(2)}) async-start(bf16[16,8,4096]{2,1,0:T(8,128)(2,1)} %get-tuple-element.385), calls=%async_computation.1 | async-start | bytes 2097152 | tf_op jit(solution)/shard_map/all_to_all | solution.py:139
  59.6 489.8 %reduce-scatter.3.cloned.1.call-start = ((), (), s32[]{:S(2)}) async-start(), calls=%async_computation.4 | async-start | bytes 4456448 | tf_op jit(solution)/shard_map/reduce_scatter | solution.py:160
  171.6 1.0 copy-start.8
  171.6 1.3 copy-start.11
  191.4 1.3 copy-start.1
  197.8 0.8 copy-start.3
  211.2 3.3 copy-start.5
  250.4 4.3 copy-start.6
  254.8 1.0 copy-start.10
  254.8 1.8 copy-start.13
  254.8 2.0 copy-start.17
  255.4 3.2 copy-start.4
  257.0 1.4 copy-start.14
  257.0 1.7 copy-start.18
  263.3 21.9 %copy-start.2 = (bf16[8,4,8,8,264]{4,2,3,1,0:T(8,128)(2,1)S(1)}, bf16[8,4,8,8,264]{4,2,3,1,0:T(8,128)(2,1)}, u32[]{:S(2)}) copy-start(bf16[8,4,8,8,264]{4,2,3,1,0:T(8,128)(2,1)} %fusion.81) | copy-start | bytes 3244036 | tf_op jit(solution)/shard_map/while
  263.3 21.9 %copy-start.7 = (bf16[8,8,32,128]{3,1,2,0:T(8,128)(2,1)S(1)}, bf16[8,8,32,128]{3,1,2,0:T(8,128)(2,1)}, u32[]{:S(2)}) copy-start(bf16[8,8,32,128]{3,1,2,0:T(8,128)(2,1)} %copy-done.6) | copy-start | bytes 1572868 | tf_op jit(solution)/shard_map/while
  289.6 21.8 %copy-start.9 = (bf16[2,8,8,4096]{3,2,1,0:T(8,128)(2,1)S(1)}, bf16[2,8,8,4096]{3,2,1,0:T(8,128)(2,1)}, u32[]{:S(2)}) copy-start(bf16[2,8,8,4096]{3,2,1,0:T(8,128)(2,1)} %copy-done.8) | copy-start | bytes 3145732 | tf_op jit(solution)/shard_map/while
  289.6 21.8 %copy-start.12 = (bf16[2,8,8,4096]{3,2,1,0:T(8,128)(2,1)S(1)}, bf16[2,8,8,4096]{3,2,1,0:T(8,128)(2,1)}, u32[]{:S(2)}) copy-start(bf16[2,8,8,4096]{3,2,1,0:T(8,128)(2,1)} %copy-done.11) | copy-start | bytes 3145732 | tf_op jit(solution)/shard_map/while
  311.4 1.0 copy-start.8
  311.4 1.3 copy-start.11
  331.3 1.3 copy-start.1
  337.6 0.8 copy-start.3
  351.0 3.3 copy-start.5
  390.3 4.3 copy-start.6
  394.6 1.0 copy-start.10
  394.6 1.8 copy-start.13
  394.6 2.0 copy-start.17
  395.3 3.2 copy-start.4
  396.8 1.4 copy-start.14
  396.8 1.7 copy-start.18
  403.1 21.9 %copy-start.2 = (bf16[8,4,8,8,264]{4,2,3,1,0:T(8,128)(2,1)S(1)}, bf16[8,4,8,8,264]{4,2,3,1,0:T(8,128)(2,1)}, u32[]{:S(2)}) copy-start(bf16[8,4,8,8,264]{4,2,3,1,0:T(8,128)(2,1)} %fusion.81) | copy-start | bytes 3244036 | tf_op jit(solution)/shard_map/while
  403.1 21.9 %copy-start.7 = (bf16[8,8,32,128]{3,1,2,0:T(8,128)(2,1)S(1)}, bf16[8,8,32,128]{3,1,2,0:T(8,128)(2,1)}, u32[]{:S(2)}) copy-start(bf16[8,8,32,128]{3,1,2,0:T(8,128)(2,1)} %copy-done.6) | copy-start | bytes 1572868 | tf_op jit(solution)/shard_map/while
  429.4 21.8 %copy-start.9 = (bf16[2,8,8,4096]{3,2,1,0:T(8,128)(2,1)S(1)}, bf16[2,8,8,4096]{3,2,1,0:T(8,128)(2,1)}, u32[]{:S(2)}) copy-start(bf16[2,8,8,4096]{3,2,1,0:T(8,128)(2,1)} %copy-done.8) | copy-start | bytes 3145732 | tf_op jit(solution)/shard_map/while
  429.4 21.8 %copy-start.12 = (bf16[2,8,8,4096]{3,2,1,0:T(8,128)(2,1)S(1)}, bf16[2,8,8,4096]{3,2,1,0:T(8,128)(2,1)}, u32[]{:S(2)}) copy-start(bf16[2,8,8,4096]{3,2,1,0:T(8,128)(2,1)} %copy-done.11) | copy-start | bytes 3145732 | tf_op jit(solution)/shard_map/while
  451.3 1.6 copy-start.15
  451.3 203.0 %reduce-scatter.5.cloned.1.call-start = ((), (), s32[]{:S(2)}) async-start(), calls=%async_computation.5 | async-start | bytes 4456448 | tf_op jit(solution)/shard_map/reduce_scatter | solution.py:161
Sparse Core Ops, SparseCore 0:
  10.7 78.2 all-gather.4
  91.8 74.8 all-gather.6
  451.4 98.0 reduce-scatter.2
  554.3 99.9 reduce-scatter.4
where the time goes:
time: 741 us; the launch traced here: 739 us
  waiting for transfers between devices  331 us (45%)
  local copies, waits for them, and re-layouts  146 us (20%)
  other arithmetic  123 us (17%)
  blocking collectives  75.4 us (10%)
  matrix products  25.9 us (3%)
  starting transfers between devices  22.4 us (3%)
  between operations  13.9 us (2%)
    reduce_scatter x1, waiting for transfers between devices, local(): lax.psum_scatter(totals[1], 'ctx', scatter_dimension=0, tiled=True)  103 us
    reduce_scatter x1, waiting for transfers between devices, local(): lax.psum_scatter(totals[0], 'ctx', scatter_dimension=0, tiled=True)  95.5 us
    gather x96, local copies, waits for them, and re-layouts  83.9 us
    all_gather x1, waiting for transfers between devices, local(): lax.all_gather(value_rows, 'ctx', axis=0, tiled=True)  77.6 us
    psum x1, blocking collectives, local(): lax.psum((jnp.sum(query_grads, axis=(0, 1)), jnp.sum(key_grad, axis=0), j...  75.4 us
    scatter-add x2, other arithmetic, group_step(): key_total = totals[0].at[rows_hit].add(key_grad.reshape(-1, key_cols))  43.7 us
    scatter-add x2, other arithmetic, group_step(): value_total = totals[1].at[rows_hit].add(value_grad.reshape(-1, key_cols))  43.6 us
    all_to_all x1, waiting for transfers between devices, local(): lax.all_to_all(send_dout, 'ctx', split_axis=0, concat_axis=0, tiled=True)  25.8 us
  transfers between devices with their start and end apart: 6, of which 6 were waited for; matrix products, arithmetic and copies ran while one was open for 1% of the time, Pallas kernels for 0%

commit v1 on v0

v1 whole, which is shorter than its diff:
```python
import math

import jax
import jax.numpy as jnp
from jax import lax
from jax.experimental import pallas as pl
from jax.experimental.pallas import tpu as pltpu
from jax.sharding import PartitionSpec as P

HD = 128
HQ = 32
HK = 4
GROUP = HQ // HK
ROWS = 128
WIN = 384
BLK = 8
N = 16
MESH = pl.DeviceIdType.MESH
NT = (((1,), (1,)), ((), ()))
SCALE = 1.0 / math.sqrt(HD)
LOG2E = math.log2(math.e)
SLICES = HK + 1


def dot(a, b):
    return jnp.dot(a, b, preferred_element_type=jnp.float32)


def dot_nt(a, b):
    return lax.dot_general(a, b, NT, preferred_element_type=jnp.float32)


def halves(x):
    high = x.astype(jnp.bfloat16)
    return high, (x - high.astype(jnp.float32)).astype(jnp.bfloat16)


def kernel(
    len_ref, place_ref, q_ref, k_ref, v_ref, do_ref,
    rows_ref, gk_ref, gv_ref, bias_ref,
    win, send, perm, mask, probs, dscore, ones, part, part_in, own, colsum, bvec, b1, b2, btot,
    halo_s, halo_r, a2a_s, a2a_r, loc_s, part_s, part_r, p1_s, p1_r, p2_s, p2_r, p3_s, p3_r,
):
    me = lax.axis_index("ctx")
    seq = lax.axis_index("dp")
    half = me // 8
    inner = lax.rem(me, 8)

    peers = [(1 - half) * 8 + lax.rem(inner + j, 8) for j in range(8)]
    peers += [half * 8 + lax.rem(inner + j, 8) for j in range(1, 8)]
    seqs = [lax.rem(seq + j, N) for j in range(1, N)]

    def remote(src, dst, send_sem, recv_sem, device):
        return pltpu.make_async_remote_copy(
            src_ref=src, dst_ref=dst, send_sem=send_sem, recv_sem=recv_sem,
            device_id=device, device_id_type=MESH,
        )

    barrier = pltpu.get_barrier_semaphore()
    for p in peers:
        pl.semaphore_signal(barrier, inc=1, device_id={"ctx": p}, device_id_type=MESH)
    for s in seqs:
        pl.semaphore_signal(barrier, inc=1, device_id={"dp": s}, device_id_type=MESH)

    for g in range(HK):
        win[g, 2, 0] = k_ref[:, g * HD : (g + 1) * HD]
        win[g, 2, 1] = v_ref[:, g * HD : (g + 1) * HD]

    @pl.when(me < 2)
    def _():
        win[:, 0] = jnp.zeros((HK, 2, ROWS, HD), jnp.bfloat16)

    @pl.when(me < 1)
    def _():
        win[:, 1] = jnp.zeros((HK, 2, ROWS, HD), jnp.bfloat16)

    lane = lax.broadcasted_iota(jnp.int32, (1, ROWS), 1)
    pos = me * ROWS + lane
    first = jnp.zeros((1, ROWS), jnp.int32)
    start = len_ref[0, 0] * 0
    for i in range(N):
        first = jnp.where(pos >= start, start, first)
        start = start + len_ref[0, i]
    t_pos = (me - 2) * ROWS + lax.broadcasted_iota(jnp.int32, (WIN, ROWS), 0)
    seen = (t_pos >= first) & (t_pos <= pos)
    mask[...] = jnp.where(seen, 0.0, -1e30)

    target = lax.rem(lane, BLK)
    for j in range(N):
        target = target + jnp.where(lane // BLK == j, place_ref[0, me, j] * BLK, 0)
    row = lax.broadcasted_iota(jnp.int32, (ROWS, ROWS), 0)
    perm[...] = jnp.where(row == target, 1.0, 0.0).astype(jnp.bfloat16)
    ones[...] = jnp.where(
        lax.broadcasted_iota(jnp.int32, (GROUP * ROWS, HD), 0) // ROWS
        == lax.broadcasted_iota(jnp.int32, (GROUP * ROWS, HD), 1),
        1.0, 0.0,
    ).astype(jnp.bfloat16)

    pl.semaphore_wait(barrier, len(peers) + len(seqs))

    def halo(g, slot):
        return remote(
            win.at[g, 2], win.at[g, slot], halo_s.at[g, slot], halo_r.at[g, slot],
            {"ctx": lax.rem(me + (2 - slot), N)},
        )

    def term(g, slot):
        return remote(
            part.at[g, slot], part_in.at[g, slot], part_s.at[g, slot], part_r.at[g, slot],
            {"ctx": lax.rem(me + N - (2 - slot), N)},
        )

    for g in range(HK):
        for slot in (1, 0):

            @pl.when(me + (2 - slot) < N)
            def _():
                halo(g, slot).start()

    def placed(g, p):
        cols = pl.ds(pl.multiple_of(g * GROUP * HD, GROUP * HD), GROUP * HD)
        return remote(
            send.at[p, :, :, cols], rows_ref.at[me, :, :, cols], a2a_s.at[g, p], a2a_r.at[g, me],
            {"ctx": p},
        )

    def arrived(g, p):
        cols = pl.ds(pl.multiple_of(g * GROUP * HD, GROUP * HD), GROUP * HD)
        return remote(
            send.at[p, :, :, cols], rows_ref.at[p, :, :, cols], a2a_s.at[g, p], a2a_r.at[g, p],
            {"ctx": p},
        )

    def kept(g):
        cols = pl.ds(pl.multiple_of(g * GROUP * HD, GROUP * HD), GROUP * HD)
        return pltpu.make_async_copy(
            send.at[me, :, :, cols], rows_ref.at[me, :, :, cols], loc_s.at[g]
        )

    def to_owner(s):
        return remote(bvec.at[s], b1.at[me], p1_s.at[s], p1_r.at[me], {"ctx": s})

    def group_step(g, carry):
        for slot in (1, 0):

            @pl.when(me >= 2 - slot)
            def _():
                halo(g, slot).wait_recv()

        keys = win[g, :, 0].reshape(WIN, HD)
        values = win[g, :, 1].reshape(WIN, HD)
        keys_t = keys.astype(jnp.float32).T.astype(jnp.bfloat16)
        values_t = values.astype(jnp.float32).T.astype(jnp.bfloat16)
        shut = jnp.concatenate([mask[...], mask[...]], axis=1)

        def stacked(ref, first_head, count):
            cols = pl.ds(pl.multiple_of((g * GROUP + first_head) * HD, HD), count * HD)
            x = ref[:, cols]
            return jnp.concatenate([x[:, i * HD : (i + 1) * HD] for i in range(count)], axis=0)

        for pair in range(GROUP // 2):
            q2 = stacked(q_ref, pair * 2, 2)
            do2 = stacked(do_ref, pair * 2, 2)
            scores = dot_nt(keys, q2) + shut
            top = jnp.max(scores, axis=0, keepdims=True)
            e = jnp.exp2((scores - top) * (SCALE * LOG2E))
            inv = 1.0 / jnp.sum(e, axis=0, keepdims=True)
            weights = (e * inv).astype(jnp.bfloat16)
            grad = dot_nt(values, do2)
            delta = jnp.sum(weights.astype(jnp.float32) * grad, axis=0, keepdims=True)
            ds = (e * (inv * SCALE) * (grad - delta)).astype(jnp.bfloat16)
            at = slice(pair * 2 * ROWS, (pair + 1) * 2 * ROWS)
            probs[:, at] = weights
            dscore[:, at] = ds
            cols = pl.ds(pl.multiple_of((g * GROUP + pair * 2) * HD, 2 * HD), 2 * HD)
            for i, out_t in enumerate((dot(values_t, weights), dot(keys_t, ds))):
                out_t = out_t.astype(jnp.bfloat16)
                out = dot_nt(
                    perm[...], jnp.concatenate([out_t[:, :ROWS], out_t[:, ROWS:]], axis=0)
                )
                send[:, i, :, cols] = out.reshape(N, BLK, 2 * HD).astype(jnp.bfloat16)

        for p in peers:
            placed(g, p).start()
        kept(g).start()

        dv = dot(probs[...], stacked(do_ref, 0, GROUP))
        both = jnp.concatenate([stacked(q_ref, 0, GROUP), ones[...]], axis=1)
        dk = dot(dscore[...], both)
        part[g, :, 0] = dk[: 2 * ROWS, :HD].reshape(2, ROWS, HD).astype(jnp.bfloat16)
        part[g, :, 1] = dv[: 2 * ROWS].reshape(2, ROWS, HD).astype(jnp.bfloat16)
        for slot in (1, 0):

            @pl.when(me >= 2 - slot)
            def _():
                term(g, slot).start()

        own[g, 0] = dk[2 * ROWS :, :HD]
        own[g, 1] = dv[2 * ROWS :]
        colsum[g, 0] = jnp.broadcast_to(jnp.sum(dk[:, :HD], axis=0, keepdims=True), (8, HD))
        colsum[g, 1] = jnp.broadcast_to(jnp.sum(dv, axis=0, keepdims=True), (8, HD))
        high, low = halves(dk[:, HD:])
        query_sum = dot(keys_t, high) + dot(keys_t, low)
        bvec[g] = query_sum.T[:GROUP]

        @pl.when(me != g)
        def _():
            to_owner(g).start()

        return carry

    lax.fori_loop(0, HK, group_step, 0)

    for g in range(HK):
        bvec[HK, g : g + 1] = colsum[g, 0, :1]
        bvec[HK, HK + g : HK + g + 1] = colsum[g, 1, :1]

    @pl.when(me != HK)
    def _():
        to_owner(HK).start()

    def spread(j):
        s = seqs[j]
        return remote(b2.at[0], b2.at[1 + j], p2_s.at[j], p2_r.at[j], {"dp": s})

    def to_all(j, p):
        return remote(btot.at[me], btot.at[me], p3_s.at[j], p3_r.at[me], {"ctx": p})

    @pl.when(me < SLICES)
    def _():
        total = bvec[me]
        for p in peers:
            remote(bvec.at[me], b1.at[p], p1_s.at[me], p1_r.at[p], {"ctx": p}).wait_recv()
        for p in peers:
            total = total + b1[p]
        b2[0] = total
        for j in range(N - 1):
            spread(j).start()
        for j in range(N - 1):
            spread(j).wait_recv()
        rank = [lax.rem(s + N - seq, N) for s in range(N)]
        total = b2[rank[0]]
        for s in range(1, N):
            total = total + b2[rank[s]]
        btot[me] = total
        for j, p in enumerate(peers):
            to_all(j, p).start()

    for s in range(SLICES):

        @pl.when(me != s)
        def _():
            remote(btot.at[s], btot.at[s], p3_s.at[0], p3_r.at[s], {"ctx": s}).wait_recv()

    bias_ref[...] = btot[...]

    for g in range(HK):
        for slot in (1, 0):

            @pl.when(me + (2 - slot) < N)
            def _():
                term(g, slot).wait_recv()

            @pl.when(me + (2 - slot) >= N)
            def _():
                part_in[g, slot] = jnp.zeros((2, ROWS, HD), jnp.bfloat16)

        for i, ref in enumerate((gk_ref, gv_ref)):
            total = own[g, i] + part_in[g, 1, i].astype(jnp.float32)
            total = total + part_in[g, 0, i].astype(jnp.float32)
            ref[:, g * HD : (g + 1) * HD] = total.astype(jnp.bfloat16)

    def finish(g, carry):
        for slot in (1, 0):

            @pl.when(me + (2 - slot) < N)
            def _():
                halo(g, slot).wait_send()

            @pl.when(me >= 2 - slot)
            def _():
                term(g, slot).wait_send()

        @pl.when(me != g)
        def _():
            to_owner(g).wait_send()

        for p in peers:
            placed(g, p).wait_send()
        kept(g).wait()
        for p in peers:
            arrived(g, p).wait_recv()
        return carry

    lax.fori_loop(0, HK, finish, 0)

    @pl.when(me != HK)
    def _():
        to_owner(HK).wait_send()

    @pl.when(me < SLICES)
    def _():
        for j in range(N - 1):
            spread(j).wait_send()
        for j, p in enumerate(peers):
            to_all(j, p).wait_send()


def local(queries, keys, values, grad_out, doc_lengths, placement):
    smem = pl.BlockSpec(memory_space=pltpu.SMEM)
    vmem = pl.BlockSpec(memory_space=pltpu.VMEM)
    bf16, f32 = jnp.bfloat16, jnp.float32
    dma = pltpu.SemaphoreType.DMA
    rows, grad_k, grad_v, bias = pl.pallas_call(
        kernel,
        out_shape=(
            jax.ShapeDtypeStruct((N, 2, BLK, HQ * HD), bf16),
            jax.ShapeDtypeStruct((ROWS, HK * HD), bf16),
            jax.ShapeDtypeStruct((ROWS, HK * HD), bf16),
            jax.ShapeDtypeStruct((SLICES, 8, HD), f32),
        ),
        in_specs=[smem, smem, vmem, vmem, vmem, vmem],
        out_specs=(pl.BlockSpec(memory_space=pl.ANY), vmem, vmem, vmem),
        scratch_shapes=[
            pltpu.VMEM((HK, 3, 2, ROWS, HD), bf16),
            pltpu.VMEM((N, 2, BLK, HQ * HD), bf16),
            pltpu.VMEM((ROWS, ROWS), bf16),
            pltpu.VMEM((WIN, ROWS), f32),
            pltpu.VMEM((WIN, GROUP * ROWS), bf16),
            pltpu.VMEM((WIN, GROUP * ROWS), bf16),
            pltpu.VMEM((GROUP * ROWS, HD), bf16),
            pltpu.VMEM((HK, 2, 2, ROWS, HD), bf16),
            pltpu.VMEM((HK, 2, 2, ROWS, HD), bf16),
            pltpu.VMEM((HK, 2, ROWS, HD), f32),
            pltpu.VMEM((HK, 2, 8, HD), f32),
            pltpu.VMEM((SLICES, 8, HD), f32),
            pltpu.VMEM((N, 8, HD), f32),
            pltpu.VMEM((N, 8, HD), f32),
            pltpu.VMEM((SLICES, 8, HD), f32),
            dma((HK, 2)), dma((HK, 2)),
            dma((HK, N)), dma((HK, N)), dma((HK,)),
            dma((HK, 2)), dma((HK, 2)),
            dma((SLICES,)), dma((N,)),
            dma((N,)), dma((N,)),
            dma((N,)), dma((SLICES,)),
        ],
        compiler_params=pltpu.CompilerParams(
            collective_id=0, has_side_effects=True, vmem_limit_bytes=48 * 1024 * 1024
        ),
        cost_estimate=pl.CostEstimate(
            flops=2 * 6 * ROWS * HQ * HD * WIN,
            bytes_accessed=6 * 1024 * 1024,
            transcendentals=ROWS * HQ * WIN,
        ),
    )(doc_lengths, placement, queries[0], keys[0], values[0], grad_out[0])
    return (
        rows[:, 0].reshape(1, ROWS, HQ * HD),
        rows[:, 1].reshape(1, ROWS, HQ * HD),
        grad_k[None],
        grad_v[None],
        bias.reshape(SLICES * 8 * HD),
    )


def solution(mesh):
    return jax.shard_map(
        local,
        mesh=mesh,
        in_specs=(
            P("dp", "ctx", None),
            P("dp", "ctx", None),
            P("dp", "ctx", None),
            P("dp", "ctx", None),
            P("dp", None),
            P("dp", None, None),
        ),
        out_specs=(
            P("dp", "ctx", None),
            P("dp", "ctx", None),
            P("dp", "ctx", None),
            P("dp", "ctx", None),
            P(),
        ),
        check_vma=False,
    )
```

time: 741 us -> 112 us (0.15)
  waiting for transfers between devices: 331 us -> 0 us
  local copies, waits for them, and re-layouts: 146 us -> 8.97 us
  other arithmetic: 123 us -> 0 us
  Pallas kernels: 0 us -> 102 us
  blocking collectives: 75.4 us -> 0 us
  matrix products: 25.9 us -> 0 us
  starting transfers between devices: 22.4 us -> 0 us
  between operations: 13.9 us -> 0.66 us
    reduce_scatter x2 -> x0, waiting for transfers between devices: 199 us -> none  [the longest x1 103 us: local(): lax.psum_scatter(totals[1], 'ctx', scatter_dimension=0, tiled=True)]
    pallas_call x0 -> x1, Pallas kernels: none -> 102 us  [local(): pl.pallas_call(kernel, out_shape=(jax.ShapeDtypeStruct((N, 2, BLK, HQ * H...]
    scatter-add x4 -> x0, other arithmetic: 87.3 us -> none  [the longest x2 43.7 us: group_step(): key_total = totals[0].at[rows_hit].add(key_grad.reshape(-1, key_cols))]
    gather x98 -> x0, local copies, waits for them, and re-layouts: 86.4 us -> none
    all_gather x2 -> x0, waiting for transfers between devices: 80.6 us -> none  [the longest x1 77.6 us: local(): lax.all_gather(value_rows, 'ctx', axis=0, tiled=True)]
    psum x1 -> x0, blocking collectives: 75.4 us -> none  [local(): lax.psum((jnp.sum(query_grads, axis=(0, 1)), jnp.sum(key_grad, axis=0), j...]
    all_to_all x2 -> x0, waiting for transfers between devices: 49.6 us -> none  [the longest x1 25.8 us: local(): lax.all_to_all(send_dout, 'ctx', split_axis=0, concat_axis=0, tiled=True)]
    dot_general x12 -> x0, matrix products: 25.9 us -> none  [the longest x2 8.63 us: block_attention(): jnp.einsum('rgnd,wgd->gnrw', dout_heads, value_heads, preferred_element_t...]
  transfers between devices with their start and end apart: 6 -> 0, of which waited for: 6 -> 0; matrix products, arithmetic and copies ran while one was open for 1% -> 0% of each run, Pallas kernels for 0% -> 0%
where the time goes in v1:
time: 112 us
  Pallas kernels  102 us (91%)
  local copies, waits for them, and re-layouts  8.97 us (8%)
    pallas_call x1, Pallas kernels, local(): pl.pallas_call(kernel, out_shape=(jax.ShapeDtypeStruct((N, 2, BLK, HQ * H...  102 us
    unnamed x15, local copies, waits for them, and re-layouts  7.52 us

profile of v1, /device:TPU:1, one launch (start us, length us, event | category | flops | bytes accessed | tf_op | source)
XLA Modules:
  0.0 111.5 jit_solution(5330639354235230881)
XLA Ops:
  0.6 0.0 copy-start
  0.6 1.2 %copy-done = bf16[1,128,4096]{2,1,0:T(8,128)(2,1)S(1)} copy-done((bf16[1,128,4096]{2,1,0:T(8,128)(2,1)S(1)}, bf16[1,128,4096]{2,1,0:T(8,128)(2,1)}, u32[]{:S(2)}) %copy-start) | copy-done | bytes 1048600
  1.9 0.0 copy-start.1
  1.9 1.2 %copy-done.1 = bf16[1,128,4096]{2,1,0:T(8,128)(2,1)S(1)} copy-done((bf16[1,128,4096]{2,1,0:T(8,128)(2,1)S(1)}, bf16[1,128,4096]{2,1,0:T(8,128)(2,1)}, u32[]{:S(2)}) %copy-start.1) | copy-done | bytes 1048600
  3.1 0.0 copy-start.2
  3.1 0.9 copy-done.2
  4.0 0.0 copy-start.3
  4.0 0.9 copy-done.3
  4.9 0.0 copy-start.4
  4.9 0.7 copy-done.4
  5.6 0.0 copy-start.5
  5.6 0.7 copy-done.5
  6.2 101.9 %shard_map.101 = (bf16[16,2,8,4096]{3,2,1,0:T(8,128)(2,1)S(1)}, bf16[128,512]{1,0:T(8,128)(2,1)S(1)}, bf16[128,512]{1,0:T(8,128)(2,1)S(1)}, f32[5,8,128]{2,1,0:T(8,128)S(1)}) custom-call(s32[1,16]{1,0:T(1,128)S(1)} %copy-done.5, s32[1,16,16]{2,1,0:T(8,128)S(1)} %copy-done.4, bf16[128,4096]{1,0:T(8,128)(2,1)S(1)} %bitcast.14, bf16[128,512]{1,0:T(8,128)(2,1)S(1)} %bitcast.16, ...), custom_call_target="tpu_custom_call" | custom-call | flops 2415919104 | bytes 6291456 | tf_op jit(solution)/shard_map/pallas_call | solution.py:314
  108.1 1.5 %slice_bitcast_fusion = (bf16[1,128,4096]{2,1,0:T(8,128)(2,1)}, bf16[1,128,4096]{2,1,0:T(8,128)(2,1)}) fusion(bf16[16,2,8,4096]{3,2,1,0:T(8,128)(2,1)S(1)} %get-tuple-element.9), kind=kLoop, calls=%fused_computation | loop fusion | bytes 4194304 | tf_op jit(solution)/shard_map/reshape;squeeze | solution.py:358
  109.6 0.7 copy.14
  110.2 0.7 copy.15
  110.9 0.6 copy.16
Async XLA Ops:
  0.6 1.2 %copy-start = (bf16[1,128,4096]{2,1,0:T(8,128)(2,1)S(1)}, bf16[1,128,4096]{2,1,0:T(8,128)(2,1)}, u32[]{:S(2)}) copy-start(bf16[1,128,4096]{2,1,0:T(8,128)(2,1)} %param.6) | copy-start | bytes 3145732
  1.9 1.2 %copy-start.1 = (bf16[1,128,4096]{2,1,0:T(8,128)(2,1)S(1)}, bf16[1,128,4096]{2,1,0:T(8,128)(2,1)}, u32[]{:S(2)}) copy-start(bf16[1,128,4096]{2,1,0:T(8,128)(2,1)} %param.9) | copy-start | bytes 3145732
  3.1 0.9 copy-start.2
  4.0 0.9 copy-start.3
  4.9 0.7 copy-start.4
  5.6 0.7 copy-start.5

commit v2 on v1

v2 whole, which is shorter than its diff:
```python
import contextlib
import math

import jax
import jax.numpy as jnp
from jax import lax
from jax.experimental import pallas as pl
from jax.experimental.pallas import tpu as pltpu
from jax.sharding import PartitionSpec as P

HD = 128
HQ = 32
HK = 4
GROUP = HQ // HK
ROWS = 128
WIN = 384
BLK = 8
N = 16
MESH = pl.DeviceIdType.MESH
NT = (((1,), (1,)), ((), ()))
SCALE = 1.0 / math.sqrt(HD)
LOG2E = math.log2(math.e)
SLICES = HK + 1
FIRST_OWNER = 3
HELD = 2


SCOPES = False


def scope(name):
    return jax.named_scope(name) if SCOPES else contextlib.nullcontext()


def dot(a, b):
    return jnp.dot(a, b, preferred_element_type=jnp.float32)


def dot_nt(a, b):
    return lax.dot_general(a, b, NT, preferred_element_type=jnp.float32)


def halves(x):
    high = x.astype(jnp.bfloat16)
    return high, (x - high.astype(jnp.float32)).astype(jnp.bfloat16)


def kernel(
    len_hbm, place_hbm, q_hbm, k_hbm, v_hbm, do_hbm,
    rows_ref, bias_ref,
    len_ref, place_ref, q_ref, k_ref, v_ref, do_ref, in_s, gkv, gkv_s, win, win_relay, send, perm, mask,
    probs, dscore, ones, part, part_in, part_relay, own, colsum, bvec, b1, b2, b3, btot,
    halo_s, halo_r, relay_s, relay_r, back_s, back_r, a2a_s, a2a_r, loc_s, part_s, part_r,
    p1_s, p1_r, p2_s, p2_r, p3_s, p3_r, p4_s, p4_r,
):
    me = lax.axis_index("ctx")
    seq = lax.axis_index("dp")
    half = me // 8
    inner = lax.rem(me, 8)

    x = seq // 4
    low = lax.rem(seq, 4)
    depth = half * 4 + low
    core = lax.rem(me, 2)

    across = [(1 - half) * 8 + lax.rem(inner + j, 8) for j in range(8)]
    near = [half * 8 + lax.rem(inner + j, 8) for j in range(1, 8)]
    peers = [{"ctx": p} for p in across + near]
    along_x = [{"dp": lax.rem(x + j, 4) * 4 + low} for j in range(1, 4)]
    along_z = []
    for j in range(1, 8):
        z = lax.rem(depth + j, 8)
        along_z.append({"ctx": (z // 4) * 8 + inner, "dp": x * 4 + lax.rem(z, 4)})
    others = peers + along_x + [along_z[j - 1] for j in range(1, 8) if j != 4]

    def remote(src, dst, send_sem, recv_sem, device):
        return pltpu.make_async_remote_copy(
            src_ref=src, dst_ref=dst, send_sem=send_sem, recv_sem=recv_sem,
            device_id=device, device_id_type=MESH,
        )

    def columns(g):
        return pl.ds(pl.multiple_of(g * GROUP * HD, GROUP * HD), GROUP * HD)

    def fetch_q(g):
        return pltpu.make_async_copy(q_hbm.at[:, columns(g)], q_ref.at[:, columns(g)], in_s.at[g])

    def fetch_do(g):
        return pltpu.make_async_copy(
            do_hbm.at[:, columns(g)], do_ref.at[:, columns(g)], in_s.at[HK + g]
        )

    small = [
        pltpu.make_async_copy(src, dst, in_s.at[2 * HK + i])
        for i, (src, dst) in enumerate(
            ((k_hbm, k_ref), (v_hbm, v_ref), (len_hbm, len_ref), (place_hbm, place_ref))
        )
    ]
    with scope("signals"):
        for copy in small:
            copy.start()
        barrier = pltpu.get_barrier_semaphore()
        for device in others:
            pl.semaphore_signal(barrier, inc=1, device_id=device, device_id_type=MESH)
        for g in range(HK):
            fetch_q(g).start()
            fetch_do(g).start()
        for copy in small:
            copy.wait()

    for g in range(HK):
        win[g, 2, 0] = k_ref[:, g * HD : (g + 1) * HD]
        win[g, 2, 1] = v_ref[:, g * HD : (g + 1) * HD]

    @pl.when(me < 2)
    def _():
        win[:, 0] = jnp.zeros((HK, 2, ROWS, HD), jnp.bfloat16)

    @pl.when(me < 1)
    def _():
        win[:, 1] = jnp.zeros((HK, 2, ROWS, HD), jnp.bfloat16)

    lane = lax.broadcasted_iota(jnp.int32, (1, ROWS), 1)
    pos = me * ROWS + lane
    first = jnp.zeros((1, ROWS), jnp.int32)
    start = len_ref[0, 0] * 0
    for i in range(N):
        first = jnp.where(pos >= start, start, first)
        start = start + len_ref[0, i]
    t_pos = (me - 2) * ROWS + lax.broadcasted_iota(jnp.int32, (WIN, ROWS), 0)
    seen = (t_pos >= first) & (t_pos <= pos)
    mask[...] = jnp.where(seen, 0.0, -1e30)

    target = lax.rem(lane, BLK)
    for j in range(N):
        target = target + jnp.where(lane // BLK == j, place_ref[0, me, j] * BLK, 0)
    row = lax.broadcasted_iota(jnp.int32, (ROWS, ROWS), 0)
    perm[...] = jnp.where(row == target, 1.0, 0.0).astype(jnp.bfloat16)
    ones[...] = jnp.where(
        lax.broadcasted_iota(jnp.int32, (GROUP * ROWS, HD), 0) // ROWS
        == lax.broadcasted_iota(jnp.int32, (GROUP * ROWS, HD), 1),
        1.0, 0.0,
    ).astype(jnp.bfloat16)

    with scope("barrier"):
        pl.semaphore_wait(barrier, len(others))

    def halo(g, slot):
        return remote(
            win.at[g, 2], win.at[g, slot], halo_s.at[g, slot], halo_r.at[g, slot],
            {"ctx": lax.rem(me + (2 - slot), N)},
        )

    def term(g, slot):
        return remote(
            part.at[g, slot], part_in.at[g, slot], part_s.at[g, slot], part_r.at[g, slot],
            {"ctx": lax.rem(me + N - (2 - slot), N)},
        )

    column = inner // 2
    relay_head = HK - 1 - column

    def leaves(slot):
        return (half == 0) & (me + (2 - slot) >= 8)

    def returns(slot):
        return (half == 1) & (me - (2 - slot) < 8)

    def has_next(g, slot):
        return (me + (2 - slot) < N) & (jnp.logical_not(leaves(slot)) | (g == 0))

    def to_relay(g):
        return remote(
            win.at[g, 2], win_relay, halo_s.at[g, 0], relay_r.at[0],
            {"ctx": 2 * (HK - 1 - g) + core},
        )

    def relayed(slot):
        return remote(
            win_relay, win.at[relay_head, slot], relay_s.at[slot], halo_r.at[relay_head, slot],
            {"ctx": 6 + core + (2 - slot)},
        )

    is_relay = (half == 0) & (column < HK - 1)

    with scope("halo_start"):
        for g in range(HK):
            for slot in (1, 0):

                @pl.when(has_next(g, slot))
                def _():
                    halo(g, slot).start()

            if g > 0:

                @pl.when((half == 0) & (column == HK - 1))
                def _():
                    to_relay(g).start()

        @pl.when(is_relay)
        def _():
            to_relay(1).wait_recv()
            relayed(0).start()

            @pl.when(core == 1)
            def _():
                relayed(1).start()

    def has_before(g, slot):
        return (me >= 2 - slot) & (jnp.logical_not(returns(slot)) | (g == HK - 1))

    def term_to_relay(g, slot):
        return remote(
            part.at[g, slot], part_relay.at[slot], part_s.at[g, slot], back_r.at[slot],
            {"ctx": 8 + 2 * (HK - 1 - g) + core},
        )

    def term_relayed(slot):
        return remote(
            part_relay.at[slot], part_in.at[relay_head, slot], back_s.at[slot],
            part_r.at[relay_head, slot], {"ctx": 8 + core - (2 - slot)},
        )

    is_back_relay = (half == 1) & (column > 0)

    def placed(g, p):
        cols = columns(g)
        return remote(
            send.at[p, :, :, cols], rows_ref.at[me, :, :, cols], a2a_s.at[g, p], a2a_r.at[g, me],
            {"ctx": p},
        )

    def arrived(g, p):
        cols = columns(g)
        return remote(
            send.at[p, :, :, cols], rows_ref.at[p, :, :, cols], a2a_s.at[g, p], a2a_r.at[g, p],
            {"ctx": p},
        )

    def kept(g):
        cols = columns(g)
        return pltpu.make_async_copy(
            send.at[me, :, :, cols], rows_ref.at[me, :, :, cols], loc_s.at[g]
        )

    def to_owner(s):
        return remote(
            bvec.at[s], b1.at[inner], p1_s.at[s], p1_r.at[inner],
            {"ctx": half * 8 + s + FIRST_OWNER},
        )

    is_owner = inner >= FIRST_OWNER

    def group_step(g, carry):
        with scope("halo"):
            fetch_q(g).wait()
            fetch_do(g).wait()
            for slot in (1, 0):

                @pl.when(me >= 2 - slot)
                def _():
                    halo(g, slot).wait_recv()

        keys = win[g, :, 0].reshape(WIN, HD)
        values = win[g, :, 1].reshape(WIN, HD)
        keys_t = keys.astype(jnp.float32).T.astype(jnp.bfloat16)
        values_t = values.astype(jnp.float32).T.astype(jnp.bfloat16)
        shut = jnp.concatenate([mask[...], mask[...]], axis=1)

        def stacked(ref, first_head, count):
            cols = pl.ds(pl.multiple_of((g * GROUP + first_head) * HD, HD), count * HD)
            x = ref[:, cols]
            return jnp.concatenate([x[:, i * HD : (i + 1) * HD] for i in range(count)], axis=0)

        with scope("heads"):
            for pair in range(GROUP // 2):
                q2 = stacked(q_ref, pair * 2, 2)
                do2 = stacked(do_ref, pair * 2, 2)
                scores = dot_nt(keys, q2) + shut
                top = jnp.max(scores, axis=0, keepdims=True)
                e = jnp.exp2((scores - top) * (SCALE * LOG2E))
                inv = 1.0 / jnp.sum(e, axis=0, keepdims=True)
                weights = (e * inv).astype(jnp.bfloat16)
                grad = dot_nt(values, do2)
                delta = jnp.sum(weights.astype(jnp.float32) * grad, axis=0, keepdims=True)
                ds = (e * (inv * SCALE) * (grad - delta)).astype(jnp.bfloat16)
                at = slice(pair * 2 * ROWS, (pair + 1) * 2 * ROWS)
                probs[:, at] = weights
                dscore[:, at] = ds
                cols = pl.ds(pl.multiple_of((g * GROUP + pair * 2) * HD, 2 * HD), 2 * HD)
                for i, out_t in enumerate((dot(values_t, weights), dot(keys_t, ds))):
                    out_t = out_t.astype(jnp.bfloat16)
                    out = dot_nt(
                        perm[...], jnp.concatenate([out_t[:, :ROWS], out_t[:, ROWS:]], axis=0)
                    )
                    send[:, i, :, cols] = out.reshape(N, BLK, 2 * HD).astype(jnp.bfloat16)

        with scope("sends"):

            @pl.when((g < HELD) | jnp.logical_not(is_owner))
            def _():
                for p in across:
                    placed(g, p).start()

            for p in near:
                placed(g, p).start()
            kept(g).start()

        with scope("terms"):
            dv = dot(probs[...], stacked(do_ref, 0, GROUP))
            both = jnp.concatenate([stacked(q_ref, 0, GROUP), ones[...]], axis=1)
            dk = dot(dscore[...], both)
            part[g, :, 0] = dk[: 2 * ROWS, :HD].reshape(2, ROWS, HD).astype(jnp.bfloat16)
            part[g, :, 1] = dv[: 2 * ROWS].reshape(2, ROWS, HD).astype(jnp.bfloat16)
            for slot in (1, 0):

                @pl.when(has_before(g, slot))
                def _():
                    term(g, slot).start()

                @pl.when(returns(slot) & (g < HK - 1))
                def _():
                    term_to_relay(g, slot).start()

            own[g, 0] = dk[2 * ROWS :, :HD]
            own[g, 1] = dv[2 * ROWS :]
            colsum[g, 0] = jnp.broadcast_to(jnp.sum(dk[:, :HD], axis=0, keepdims=True), (8, HD))
            colsum[g, 1] = jnp.broadcast_to(jnp.sum(dv, axis=0, keepdims=True), (8, HD))
            high, low = halves(dk[:, HD:])
            query_sum = dot(keys_t, high) + dot(keys_t, low)
            bvec[g] = query_sum.T[:GROUP]

            @pl.when(inner != g + FIRST_OWNER)
            def _():
                to_owner(g).start()

        return carry

    lax.fori_loop(0, HK, group_step, 0)

    for g in range(HK):
        bvec[HK, g : g + 1] = colsum[g, 0, :1]
        bvec[HK, HK + g : HK + g + 1] = colsum[g, 1, :1]

    @pl.when(inner != HK + FIRST_OWNER)
    def _():
        to_owner(HK).start()

    mine = inner - FIRST_OWNER

    def to_x(j):
        return remote(b2.at[x], b2.at[x], p2_s.at[j], p2_r.at[x], along_x[j - 1])

    def from_x(j):
        at = lax.rem(x + j, 4)
        return remote(b2.at[at], b2.at[at], p2_s.at[j], p2_r.at[at], along_x[j - 1])

    def to_z(j):
        return remote(b3.at[depth], b3.at[depth], p3_s.at[j], p3_r.at[depth], along_z[j - 1])

    def from_z(j):
        at = lax.rem(depth + j, 8)
        return remote(b3.at[at], b3.at[at], p3_s.at[j], p3_r.at[at], along_z[j - 1])

    def to_near(j):
        device = {"ctx": near[j - 1]}
        return remote(btot.at[mine], btot.at[mine], p4_s.at[j], p4_r.at[mine], device)

    with scope("owner"):

        @pl.when(is_owner)
        def _():
            b1[inner] = bvec[mine]
            for j in range(1, 8):
                at = lax.rem(inner + j, 8)
                remote(
                    bvec.at[mine], b1.at[at], p1_s.at[mine], p1_r.at[at], {"ctx": near[j - 1]}
                ).wait_recv()
            total = b1[0]
            for j in range(1, 8):
                total = total + b1[j]
            b2[x] = total
            for j in range(1, 4):
                to_x(j).start()
            for j in range(1, 4):
                from_x(j).wait_recv()
            b3[depth] = (b2[0] + b2[1]) + (b2[2] + b2[3])
            for j in range(1, 8):
                to_z(j).start()
            for g in range(HELD, HK):
                for p in across:
                    placed(g, p).start()
            for j in range(1, 8):
                from_z(j).wait_recv()
            total = b3[0]
            for j in range(1, 8):
                total = total + b3[j]
            btot[mine] = total
            for j in range(1, 8):
                to_near(j).start()

    with scope("relay"):

        @pl.when(is_back_relay)
        def _():
            term_to_relay(0, 0).wait_recv()
            term_relayed(0).start()

            @pl.when(core == 0)
            def _():
                term_to_relay(0, 1).wait_recv()
                term_relayed(1).start()

    with scope("bias"):
        for s in range(SLICES):

            @pl.when(inner != s + FIRST_OWNER)
            def _():
                remote(
                    btot.at[s], btot.at[s], p4_s.at[0], p4_r.at[s],
                    {"ctx": half * 8 + s + FIRST_OWNER},
                ).wait_recv()

    bias_ref[...] = btot[...]

    with scope("gkv"):
        for g in range(HK):
            for slot in (1, 0):

                @pl.when(me + (2 - slot) < N)
                def _():
                    term(g, slot).wait_recv()

                @pl.when(me + (2 - slot) >= N)
                def _():
                    part_in[g, slot] = jnp.zeros((2, ROWS, HD), jnp.bfloat16)

            for i in range(2):
                total = own[g, i] + part_in[g, 1, i].astype(jnp.float32)
                total = total + part_in[g, 0, i].astype(jnp.float32)
                gkv[:, i, :, g * HD : (g + 1) * HD] = total.reshape(N, BLK, HD).astype(
                    jnp.bfloat16
                )
        result = pltpu.make_async_copy(gkv, rows_ref.at[:, :, :, HQ * HD :], gkv_s)
        result.start()

    def finish(g, carry):
        for slot in (1, 0):

            @pl.when(has_next(g, slot))
            def _():
                halo(g, slot).wait_send()

            @pl.when(has_before(g, slot))
            def _():
                term(g, slot).wait_send()

            @pl.when(returns(slot) & (g < HK - 1))
            def _():
                term_to_relay(g, slot).wait_send()

        @pl.when((half == 0) & (column == HK - 1) & (g > 0))
        def _():
            to_relay(g).wait_send()

        @pl.when(inner != g + FIRST_OWNER)
        def _():
            to_owner(g).wait_send()

        for p in across + near:
            placed(g, p).wait_send()
        kept(g).wait()
        for p in near + across:
            arrived(g, p).wait_recv()
        return carry

    with scope("finish"):
        lax.fori_loop(0, HK, finish, 0)
        result.wait()

    @pl.when(inner != HK + FIRST_OWNER)
    def _():
        to_owner(HK).wait_send()

    @pl.when(is_relay)
    def _():
        relayed(0).wait_send()

        @pl.when(core == 1)
        def _():
            relayed(1).wait_send()

    @pl.when(is_back_relay)
    def _():
        term_relayed(0).wait_send()

        @pl.when(core == 0)
        def _():
            term_relayed(1).wait_send()

    @pl.when(is_owner)
    def _():
        for j in range(1, 4):
            to_x(j).wait_send()
        for j in range(1, 8):
            to_z(j).wait_send()
            to_near(j).wait_send()


def local(queries, keys, values, grad_out, doc_lengths, placement):
    vmem = pl.BlockSpec(memory_space=pltpu.VMEM)
    bf16, f32 = jnp.bfloat16, jnp.float32
    dma = pltpu.SemaphoreType.DMA
    rows, bias = pl.pallas_call(
        kernel,
        out_shape=(
            jax.ShapeDtypeStruct((N, 2, BLK, (HQ + HK) * HD), bf16),
            jax.ShapeDtypeStruct((SLICES, 8, HD), f32),
        ),
        in_specs=[pl.BlockSpec(memory_space=pltpu.HBM)] * 6,
        out_specs=(pl.BlockSpec(memory_space=pl.ANY), vmem),
        scratch_shapes=[
            pltpu.SMEM((1, N), jnp.int32),
            pltpu.SMEM((1, N, N), jnp.int32),
            pltpu.VMEM((ROWS, HQ * HD), bf16),
            pltpu.VMEM((ROWS, HK * HD), bf16),
            pltpu.VMEM((ROWS, HK * HD), bf16),
            pltpu.VMEM((ROWS, HQ * HD), bf16),
            dma((2 * HK + 4,)),
            pltpu.VMEM((N, 2, BLK, HK * HD), bf16),
            dma,
            pltpu.VMEM((HK, 3, 2, ROWS, HD), bf16),
            pltpu.VMEM((2, ROWS, HD), bf16),
            pltpu.VMEM((N, 2, BLK, HQ * HD), bf16),
            pltpu.VMEM((ROWS, ROWS), bf16),
            pltpu.VMEM((WIN, ROWS), f32),
            pltpu.VMEM((WIN, GROUP * ROWS), bf16),
            pltpu.VMEM((WIN, GROUP * ROWS), bf16),
            pltpu.VMEM((GROUP * ROWS, HD), bf16),
            pltpu.VMEM((HK, 2, 2, ROWS, HD), bf16),
            pltpu.VMEM((HK, 2, 2, ROWS, HD), bf16),
            pltpu.VMEM((2, 2, ROWS, HD), bf16),
            pltpu.VMEM((HK, 2, ROWS, HD), f32),
            pltpu.VMEM((HK, 2, 8, HD), f32),
            pltpu.VMEM((SLICES, 8, HD), f32),
            pltpu.VMEM((8, 8, HD), f32),
            pltpu.VMEM((4, 8, HD), f32),
            pltpu.VMEM((8, 8, HD), f32),
            pltpu.VMEM((SLICES, 8, HD), f32),
            dma((HK, 2)), dma((HK, 2)), dma((2,)), dma((1,)), dma((2,)), dma((2,)),
            dma((HK, N)), dma((HK, N)), dma((HK,)),
            dma((HK, 2)), dma((HK, 2)),
            dma((SLICES,)), dma((8,)), dma((4,)), dma((4,)),
            dma((8,)), dma((8,)), dma((8,)), dma((SLICES,)),
        ],
        compiler_params=pltpu.CompilerParams(
            collective_id=0, has_side_effects=True, vmem_limit_bytes=60 * 1024 * 1024
        ),
        cost_estimate=pl.CostEstimate(
            flops=2 * 6 * ROWS * HQ * HD * WIN,
            bytes_accessed=6 * 1024 * 1024,
            transcendentals=ROWS * HQ * WIN,
        ),
    )(doc_lengths, placement, queries[0], keys[0], values[0], grad_out[0])
    return (
        rows[:, 0, :, : HQ * HD].reshape(1, ROWS, HQ * HD),
        rows[:, 1, :, : HQ * HD].reshape(1, ROWS, HQ * HD),
        rows[:, 0, :, HQ * HD :].reshape(1, ROWS, HK * HD),
        rows[:, 1, :, HQ * HD :].reshape(1, ROWS, HK * HD),
        bias.reshape(SLICES * 8 * HD),
    )


def solution(mesh):
    return jax.shard_map(
        local,
        mesh=mesh,
        in_specs=(
            P("dp", "ctx", None),
            P("dp", "ctx", None),
            P("dp", "ctx", None),
            P("dp", "ctx", None),
            P("dp", None),
            P("dp", None, None),
        ),
        out_specs=(
            P("dp", "ctx", None),
            P("dp", "ctx", None),
            P("dp", "ctx", None),
            P("dp", "ctx", None),
            P(),
        ),
        check_vma=False,
    )
```

time: 112 us -> 90.7 us (0.81)
  the two profiles are of different devices: /device:TPU:1 before, /device:TPU:89 now
where the time goes in v2:
time: 90.7 us; the launch traced here: 90.6 us
  Pallas kernels  84.6 us (93%)
  local copies, waits for them, and re-layouts  5.38 us (6%)
    pallas_call x1, Pallas kernels, local(): pl.pallas_call(kernel, out_shape=(jax.ShapeDtypeStruct((N, 2, BLK, (HQ +...  84.6 us
    another operation x1, local copies, waits for them, and re-layouts, local(): rows[:, 1, :, :HQ * HD].reshape(1, ROWS, HQ * HD)  3.07 us

profile of v2, /device:TPU:89, one launch (start us, length us, event | category | flops | bytes accessed | tf_op | source)
XLA Modules:
  0.0 90.6 jit_solution(12100198318524429988)
XLA Ops:
  0.6 84.6 %shard_map.101 = (bf16[16,2,8,4608]{3,2,1,0:T(8,128)(2,1)}, f32[5,8,128]{2,1,0:T(8,128)}) custom-call(s32[1,16]{1,0:T(1,128)} %len_hbm.1, s32[1,16,16]{2,1,0:T(8,128)} %place_hbm.1, bf16[128,4096]{1,0:T(8,128)(2,1)} %bitcast.14, bf16[128,512]{1,0:T(8,128)(2,1)} %bitcast.16, bf16[128,512]{1,0:T(8,128)(2,1)} %bitcast.17, bf16[128,4096]{1,0:T(8,128)(2,1)} %bitcast.15), custom_call_target="tpu_custom_call" | custom-call | flops 2415919104 | bytes 6291456 | tf_op jit(solution)/shard_map/pallas_call | solution.py:514
  85.2 0.0 copy-start
  85.2 1.7 %slice_bitcast_fusion.2 = (bf16[1,128,512]{2,1,0:T(8,128)(2,1)}, bf16[1,128,512]{2,1,0:T(8,128)(2,1)}) fusion(bf16[16,2,8,4608]{3,2,1,0:T(8,128)(2,1)} %get-tuple-element.7), kind=kLoop, calls=%fused_computation.2 | loop fusion | bytes 524288 | tf_op jit(solution)/shard_map/reshape;squeeze | solution.py:569
  86.9 3.1 %slice_bitcast_fusion = (bf16[1,128,4096]{2,1,0:T(8,128)(2,1)}, bf16[1,128,4096]{2,1,0:T(8,128)(2,1)}) fusion(bf16[16,2,8,4608]{3,2,1,0:T(8,128)(2,1)} %get-tuple-element.7), kind=kLoop, calls=%fused_computation | loop fusion | bytes 4194304 | tf_op jit(solution)/shard_map/reshape;squeeze | solution.py:567
  90.0 0.0 copy-done
  90.0 0.6 copy.12
Async XLA Ops:
  85.2 4.8 %copy-start = (f32[5,8,128]{2,1,0:T(8,128)S(1)}, f32[5,8,128]{2,1,0:T(8,128)}, u32[]{:S(2)}) copy-start(f32[5,8,128]{2,1,0:T(8,128)} %get-tuple-element.8) | copy-start | bytes 61444

commit v3 on v2

--- a/solution.py
+++ b/solution.py
@@ -22,7 +22,8 @@
 LOG2E = math.log2(math.e)
 SLICES = HK + 1
 FIRST_OWNER = 3
-HELD = 2
+HELD = 3
+EARLY = 2 * HD
 
 
 SCOPES = False
@@ -120,6 +121,70 @@
     def _():
         win[:, 1] = jnp.zeros((HK, 2, ROWS, HD), jnp.bfloat16)
 
+    with scope("barrier"):
+        pl.semaphore_wait(barrier, len(others))
+
+    def halo(g, slot):
+        return remote(
+            win.at[g, 2], win.at[g, slot], halo_s.at[g, slot], halo_r.at[g, slot],
+            {"ctx": lax.rem(me + (2 - slot), N)},
+        )
+
+    def term(g, slot):
+        return remote(
+            part.at[g, slot], part_in.at[g, slot], part_s.at[g, slot], part_r.at[g, slot],
+            {"ctx": lax.rem(me + N - (2 - slot), N)},
+        )
+
+    column = inner // 2
+    relay_head = HK - 1 - column
+
+    def leaves(slot):
+        return (half == 0) & (me + (2 - slot) >= 8)
+
+    def returns(slot):
+        return (half == 1) & (me - (2 - slot) < 8)
+
+    def has_next(g, slot):
+        return (me + (2 - slot) < N) & (jnp.logical_not(leaves(slot)) | (g == 0))
+
+    def to_relay(g):
+        return remote(
+            win.at[g, 2], win_relay, halo_s.at[g, 0], relay_r.at[0],
+            {"ctx": 2 * (HK - 1 - g) + core},
+        )
+
+    def relayed(slot):
+        return remote(
+            win_relay, win.at[relay_head, slot], relay_s.at[slot], halo_r.at[relay_head, slot],
+            {"ctx": 6 + core + (2 - slot)},
+        )
+
+    is_relay = (half == 0) & (column < HK - 1)
+
+    with scope("halo_start"):
+        for g in range(HK):
+            for slot in (1, 0):
+
+                @pl.when(has_next(g, slot))
+                def _():
+                    halo(g, slot).start()
+
+            if g > 0:
+
+                @pl.when((half == 0) & (column == HK - 1))
+                def _():
+                    to_relay(g).start()
+
+        @pl.when(is_relay)
+        def _():
+            to_relay(1).wait_recv()
+            relayed(0).start()
+
+            @pl.when(core == 1)
+            def _():
+                relayed(1).start()
+
     lane = lax.broadcasted_iota(jnp.int32, (1, ROWS), 1)
     pos = me * ROWS + lane
     first = jnp.zeros((1, ROWS), jnp.int32)
@@ -142,70 +207,6 @@
         1.0, 0.0,
     ).astype(jnp.bfloat16)
 
-    with scope("barrier"):
-        pl.semaphore_wait(barrier, len(others))
-
-    def halo(g, slot):
-        return remote(
-            win.at[g, 2], win.at[g, slot], halo_s.at[g, slot], halo_r.at[g, slot],
-            {"ctx": lax.rem(me + (2 - slot), N)},
-        )
-
-    def term(g, slot):
-        return remote(
-            part.at[g, slot], part_in.at[g, slot], part_s.at[g, slot], part_r.at[g, slot],
-            {"ctx": lax.rem(me + N - (2 - slot), N)},
-        )
-
-    column = inner // 2
-    relay_head = HK - 1 - column
-
-    def leaves(slot):
-        return (half == 0) & (me + (2 - slot) >= 8)
-
-    def returns(slot):
-        return (half == 1) & (me - (2 - slot) < 8)
-
-    def has_next(g, slot):
-        return (me + (2 - slot) < N) & (jnp.logical_not(leaves(slot)) | (g == 0))
-
-    def to_relay(g):
-        return remote(
-            win.at[g, 2], win_relay, halo_s.at[g, 0], relay_r.at[0],
-            {"ctx": 2 * (HK - 1 - g) + core},
-        )
-
-    def relayed(slot):
-        return remote(
-            win_relay, win.at[relay_head, slot], relay_s.at[slot], halo_r.at[relay_head, slot],
-            {"ctx": 6 + core + (2 - slot)},
-        )
-
-    is_relay = (half == 0) & (column < HK - 1)
-
-    with scope("halo_start"):
-        for g in range(HK):
-            for slot in (1, 0):
-
-                @pl.when(has_next(g, slot))
-                def _():
-                    halo(g, slot).start()
-
-            if g > 0:
-
-                @pl.when((half == 0) & (column == HK - 1))
-                def _():
-                    to_relay(g).start()
-
-        @pl.when(is_relay)
-        def _():
-            to_relay(1).wait_recv()
-            relayed(0).start()
-
-            @pl.when(core == 1)
-            def _():
-                relayed(1).start()
-
     def has_before(g, slot):
         return (me >= 2 - slot) & (jnp.logical_not(returns(slot)) | (g == HK - 1))
 
@@ -235,6 +236,14 @@
         return remote(
             send.at[p, :, :, cols], rows_ref.at[p, :, :, cols], a2a_s.at[g, p], a2a_r.at[g, p],
             {"ctx": p},
+        )
+
+    def early(part, p, source):
+        cols = (slice(0, EARLY), slice(EARLY, GROUP * HD))[part]
+        i = (HK, 0)[part]
+        return remote(
+            send.at[p, :, :, cols], rows_ref.at[source, :, :, cols], a2a_s.at[i, p],
+            a2a_r.at[i, source], {"ctx": p},
         )
 
     def kept(g):
@@ -250,6 +259,7 @@
         )
 
     is_owner = inner >= FIRST_OWNER
+    is_held = inner >= 2
 
     def group_step(g, carry):
         with scope("halo"):
@@ -295,12 +305,19 @@
                     )
                     send[:, i, :, cols] = out.reshape(N, BLK, 2 * HD).astype(jnp.bfloat16)
 
+                if (pair + 1) * 2 * HD == EARLY:
+
+                    @pl.when(g == 0)
+                    def _():
+                        for p in across:
+                            early(0, p, me).start()
+
         with scope("sends"):
 
-            @pl.when((g < HELD) | jnp.logical_not(is_owner))
+            @pl.when(g == 0)
             def _():
                 for p in across:
-                    placed(g, p).start()
+                    early(1, p, me).start()
 
             for p in near:
                 placed(g, p).start()
@@ -333,6 +350,11 @@
             @pl.when(inner != g + FIRST_OWNER)
             def _():
                 to_owner(g).start()
+
+        @pl.when((g > 0) & ((g < HELD) | jnp.logical_not(is_held)))
+        def _():
+            for p in across:
+                placed(g, p).start()
 
         return carry
 
@@ -387,9 +409,29 @@
             b3[depth] = (b2[0] + b2[1]) + (b2[2] + b2[3])
             for j in range(1, 8):
                 to_z(j).start()
-            for g in range(HELD, HK):
-                for p in across:
-                    placed(g, p).start()
+
+    with scope("relay"):
+
+        @pl.when(is_back_relay)
+        def _():
+            term_to_relay(0, 0).wait_recv()
+            term_relayed(0).start()
+
+            @pl.when(core == 0)
+            def _():
+                term_to_relay(0, 1).wait_recv()
+                term_relayed(1).start()
+
+    @pl.when(is_held)
+    def _():
+        for g in range(HELD, HK):
+            for p in across:
+                placed(g, p).start()
+
+    with scope("total"):
+
+        @pl.when(is_owner)
+        def _():
             for j in range(1, 8):
                 from_z(j).wait_recv()
             total = b3[0]
@@ -399,18 +441,6 @@
             for j in range(1, 8):
                 to_near(j).start()
 
-    with scope("relay"):
-
-        @pl.when(is_back_relay)
-        def _():
-            term_to_relay(0, 0).wait_recv()
-            term_relayed(0).start()
-
-            @pl.when(core == 0)
-            def _():
-                term_to_relay(0, 1).wait_recv()
-                term_relayed(1).start()
-
     with scope("bias"):
         for s in range(SLICES):
 
@@ -467,11 +497,27 @@
         def _():
             to_owner(g).wait_send()
 
-        for p in across + near:
+        kept(g).wait()
+        for p in near:
             placed(g, p).wait_send()
-        kept(g).wait()
-        for p in near + across:
+        for p in near:
             arrived(g, p).wait_recv()
+
+        @pl.when(g == 0)
+        def _():
+            for part in range(2):
+                for p in across:
+                    early(part, p, me).wait_send()
+                for p in across:
+                    early(part, p, p).wait_recv()
+
+        @pl.when(g > 0)
+        def _():
+            for p in across:
+                placed(g, p).wait_send()
+            for p in across:
+                arrived(g, p).wait_recv()
+
         return carry
 
     with scope("finish"):
@@ -505,6 +551,35 @@
         for j in range(1, 8):
             to_z(j).wait_send()
             to_near(j).wait_send()
+
+
+PARTS = 4
+
+
+def lay_out(rows_ref, bias_ref, attn_ref, gq_ref, gk_ref, gv_ref, gb_ref, held, bias, in_s, out_s):
+    wide = slice(0, HQ * HD)
+    narrow = slice(HQ * HD, (HQ + HK) * HD)
+    size = N // PARTS
+    first = [pltpu.make_async_copy(bias_ref, bias, in_s.at[PARTS])]
+    for i in range(PARTS):
+        at = slice(i * size, (i + 1) * size)
+        first.append(pltpu.make_async_copy(rows_ref.at[at], held.at[at], in_s.at[i]))
+    for copy in first:
+        copy.start()
+    first[0].wait()
+    then = [pltpu.make_async_copy(bias, gb_ref, out_s.at[PARTS, 0])]
+    then[0].start()
+    for i in range(PARTS):
+        at = slice(i * size, (i + 1) * size)
+        first[1 + i].wait()
+        for n, (which, cols, ref) in enumerate(
+            ((0, wide, attn_ref), (1, wide, gq_ref), (0, narrow, gk_ref), (1, narrow, gv_ref))
+        ):
+            copy = pltpu.make_async_copy(held.at[at, which, :, cols], ref.at[at], out_s.at[i, n])
+            copy.start()
+            then.append(copy)
+    for copy in then:
+        copy.wait()
 
 
 def local(queries, keys, values, grad_out, doc_lengths, placement):
@@ -548,7 +623,7 @@
             pltpu.VMEM((8, 8, HD), f32),
             pltpu.VMEM((SLICES, 8, HD), f32),
             dma((HK, 2)), dma((HK, 2)), dma((2,)), dma((1,)), dma((2,)), dma((2,)),
-            dma((HK, N)), dma((HK, N)), dma((HK,)),
+            dma((HK + 1, N)), dma((HK + 1, N)), dma((HK,)),
             dma((HK, 2)), dma((HK, 2)),
             dma((SLICES,)), dma((8,)), dma((4,)), dma((4,)),
             dma((8,)), dma((8,)), dma((8,)), dma((SLICES,)),
@@ -562,12 +637,33 @@
             transcendentals=ROWS * HQ * WIN,
         ),
     )(doc_lengths, placement, queries[0], keys[0], values[0], grad_out[0])
+    shape = jax.ShapeDtypeStruct
+    results = pl.pallas_call(
+        lay_out,
+        out_shape=(
+            shape((N, BLK, HQ * HD), bf16),
+            shape((N, BLK, HQ * HD), bf16),
+            shape((N, BLK, HK * HD), bf16),
+            shape((N, BLK, HK * HD), bf16),
+            shape((SLICES, 8, HD), f32),
+        ),
+        in_specs=[pl.BlockSpec(memory_space=pl.ANY)] * 2,
+        out_specs=(pl.BlockSpec(memory_space=pl.ANY),) * 5,
+        scratch_shapes=[
+            pltpu.VMEM((N, 2, BLK, (HQ + HK) * HD), bf16),
+            pltpu.VMEM((SLICES, 8, HD), f32),
+            dma((PARTS + 1,)),
+            dma((PARTS + 1, 4)),
+        ],
+        compiler_params=pltpu.CompilerParams(vmem_limit_bytes=60 * 1024 * 1024),
+        cost_estimate=pl.CostEstimate(flops=0, bytes_accessed=5 * 1024 * 1024, transcendentals=0),
+    )(rows, bias)
     return (
-        rows[:, 0, :, : HQ * HD].reshape(1, ROWS, HQ * HD),
-        rows[:, 1, :, : HQ * HD].reshape(1, ROWS, HQ * HD),
-        rows[:, 0, :, HQ * HD :].reshape(1, ROWS, HK * HD),
-        rows[:, 1, :, HQ * HD :].reshape(1, ROWS, HK * HD),
-        bias.reshape(SLICES * 8 * HD),
+        results[0].reshape(1, ROWS, HQ * HD),
+        results[1].reshape(1, ROWS, HQ * HD),
+        results[2].reshape(1, ROWS, HK * HD),
+        results[3].reshape(1, ROWS, HK * HD),
+        results[4].reshape(SLICES * 8 * HD),
     )
 
 

time: 90.7 us -> 78.4 us (0.86)
  the two profiles are of different devices: /device:TPU:89 before, /device:TPU:1 now
where the time goes in v3:
time: 78.4 us; the launch traced here: 78.3 us
  Pallas kernels  77.7 us (99%)
    pallas_call x1, Pallas kernels, local(): pl.pallas_call(kernel, out_shape=(jax.ShapeDtypeStruct((N, 2, BLK, (HQ +...  75 us
    pallas_call x1, Pallas kernels, local(): pl.pallas_call(lay_out, out_shape=(shape((N, BLK, HQ * HD), bf16), shape(...  2.68 us

profile of v3, /device:TPU:1, one launch (start us, length us, event | category | flops | bytes accessed | tf_op | source)
XLA Modules:
  0.0 78.3 jit_solution(11628270927055286956)
XLA Ops:
  0.6 75.0 %shard_map.101 = (bf16[16,2,8,4608]{3,2,1,0:T(8,128)(2,1)}, f32[5,8,128]{2,1,0:T(8,128)}) custom-call(s32[1,16]{1,0:T(1,128)} %len_hbm.1, s32[1,16,16]{2,1,0:T(8,128)} %place_hbm.1, bf16[128,4096]{1,0:T(8,128)(2,1)} %bitcast.9, bf16[128,512]{1,0:T(8,128)(2,1)} %bitcast.13, bf16[128,512]{1,0:T(8,128)(2,1)} %bitcast.14, bf16[128,4096]{1,0:T(8,128)(2,1)} %bitcast.10), custom_call_target="tpu_custom_call" | custom-call | flops 2415919104 | bytes 6291456 | tf_op jit(solution)/shard_map/pallas_call | solution.py:589
  75.6 2.7 %shard_map.102 = (bf16[16,8,4096]{2,1,0:T(8,128)(2,1)}, bf16[16,8,4096]{2,1,0:T(8,128)(2,1)}, bf16[16,8,512]{2,1,0:T(8,128)(2,1)}, bf16[16,8,512]{2,1,0:T(8,128)(2,1)}, f32[5,8,128]{2,1,0:T(8,128)}) custom-call(bf16[16,2,8,4608]{3,2,1,0:T(8,128)(2,1)} %get-tuple-element.12.rows_ref, f32[5,8,128]{2,1,0:T(8,128)} %get-tuple-element.13.bias_ref), custom_call_target="tpu_custom_call" | custom-call | bytes 5242880 | tf_op jit(solution)/shard_map/pallas_call | solution.py:641

commit v4 on v3

--- a/solution.py
+++ b/solution.py
@@ -23,6 +23,7 @@
 SLICES = HK + 1
 FIRST_OWNER = 3
 HELD = 3
+KEEP = 4
 EARLY = 2 * HD
 
 
@@ -51,7 +52,7 @@
     rows_ref, bias_ref,
     len_ref, place_ref, q_ref, k_ref, v_ref, do_ref, in_s, gkv, gkv_s, win, win_relay, send, perm, mask,
     probs, dscore, ones, part, part_in, part_relay, own, colsum, bvec, b1, b2, b3, btot,
-    halo_s, halo_r, relay_s, relay_r, back_s, back_r, a2a_s, a2a_r, loc_s, part_s, part_r,
+    halo_s, halo_r, pass_s, relay_s, relay_r, back_s, back_r, a2a_s, a2a_r, loc_s, part_s, part_r,
     p1_s, p1_r, p2_s, p2_r, p3_s, p3_r, p4_s, p4_r,
 ):
     me = lax.axis_index("ctx")
@@ -146,7 +147,8 @@
         return (half == 1) & (me - (2 - slot) < 8)
 
     def has_next(g, slot):
-        return (me + (2 - slot) < N) & (jnp.logical_not(leaves(slot)) | (g == 0))
+        direct = jnp.logical_not(leaves(slot)) | ((g == 0) & (inner == 6 + slot))
+        return (me + (2 - slot) < N) & direct
 
     def to_relay(g):
         return remote(
@@ -154,10 +156,15 @@
             {"ctx": 2 * (HK - 1 - g) + core},
         )
 
-    def relayed(slot):
-        return remote(
-            win_relay, win.at[relay_head, slot], relay_s.at[slot], halo_r.at[relay_head, slot],
-            {"ctx": 6 + core + (2 - slot)},
+    def relayed():
+        return remote(
+            win_relay, win.at[relay_head, core], relay_s.at[0], halo_r.at[relay_head, core],
+            {"ctx": 8},
+        )
+
+    def handed(g):
+        return remote(
+            win.at[g, 1], win.at[g, 0], pass_s.at[g], halo_r.at[g, 0], {"ctx": 9}
         )
 
     is_relay = (half == 0) & (column < HK - 1)
@@ -179,11 +186,7 @@
         @pl.when(is_relay)
         def _():
             to_relay(1).wait_recv()
-            relayed(0).start()
-
-            @pl.when(core == 1)
-            def _():
-                relayed(1).start()
+            relayed().start()
 
     lane = lax.broadcasted_iota(jnp.int32, (1, ROWS), 1)
     pos = me * ROWS + lane
@@ -271,6 +274,12 @@
                 def _():
                     halo(g, slot).wait_recv()
 
+                if slot == 1:
+
+                    @pl.when(me == 8)
+                    def _():
+                        handed(g).start()
+
         keys = win[g, :, 0].reshape(WIN, HD)
         values = win[g, :, 1].reshape(WIN, HD)
         keys_t = keys.astype(jnp.float32).T.astype(jnp.bfloat16)
@@ -283,15 +292,20 @@
             return jnp.concatenate([x[:, i * HD : (i + 1) * HD] for i in range(count)], axis=0)
 
         with scope("heads"):
-            for pair in range(GROUP // 2):
+            def products(pair):
                 q2 = stacked(q_ref, pair * 2, 2)
                 do2 = stacked(do_ref, pair * 2, 2)
-                scores = dot_nt(keys, q2) + shut
+                return dot_nt(keys, q2) + shut, dot_nt(values, do2)
+
+            ahead = products(0)
+            for pair in range(GROUP // 2):
+                scores, grad = ahead
+                if pair + 1 < GROUP // 2:
+                    ahead = products(pair + 1)
                 top = jnp.max(scores, axis=0, keepdims=True)
                 e = jnp.exp2((scores - top) * (SCALE * LOG2E))
                 inv = 1.0 / jnp.sum(e, axis=0, keepdims=True)
                 weights = (e * inv).astype(jnp.bfloat16)
-                grad = dot_nt(values, do2)
                 delta = jnp.sum(weights.astype(jnp.float32) * grad, axis=0, keepdims=True)
                 ds = (e * (inv * SCALE) * (grad - delta)).astype(jnp.bfloat16)
                 at = slice(pair * 2 * ROWS, (pair + 1) * 2 * ROWS)
@@ -319,9 +333,11 @@
                 for p in across:
                     early(1, p, me).start()
 
-            for p in near:
-                placed(g, p).start()
-            kept(g).start()
+            @pl.when((g > 0) & ((g < HELD) | jnp.logical_not(is_held | (half == 1))))
+            def _():
+                for p in across:
+                    placed(g, p).start()
+
 
         with scope("terms"):
             dv = dot(probs[...], stacked(do_ref, 0, GROUP))
@@ -351,11 +367,19 @@
             def _():
                 to_owner(g).start()
 
-        @pl.when((g > 0) & ((g < HELD) | jnp.logical_not(is_held)))
-        def _():
-            for p in across:
+        @pl.when((g >= HELD) & jnp.logical_not(is_held) & (half == 1))
+        def _():
+            for p in across[:KEEP]:
                 placed(g, p).start()
 
+        @pl.when((g >= HELD) & (is_held | (half == 1)))
+        def _():
+            for p in across[KEEP:]:
+                placed(g, p).start()
+
+        for p in near:
+            placed(g, p).start()
+        kept(g).start()
         return carry
 
     lax.fori_loop(0, HK, group_step, 0)
@@ -425,7 +449,7 @@
     @pl.when(is_held)
     def _():
         for g in range(HELD, HK):
-            for p in across:
+            for p in across[:KEEP]:
                 placed(g, p).start()
 
     with scope("total"):
@@ -493,6 +517,10 @@
         def _():
             to_relay(g).wait_send()
 
+        @pl.when(me == 8)
+        def _():
+            handed(g).wait_send()
+
         @pl.when(inner != g + FIRST_OWNER)
         def _():
             to_owner(g).wait_send()
@@ -530,11 +558,7 @@
 
     @pl.when(is_relay)
     def _():
-        relayed(0).wait_send()
-
-        @pl.when(core == 1)
-        def _():
-            relayed(1).wait_send()
+        relayed().wait_send()
 
     @pl.when(is_back_relay)
     def _():
@@ -622,7 +646,7 @@
             pltpu.VMEM((4, 8, HD), f32),
             pltpu.VMEM((8, 8, HD), f32),
             pltpu.VMEM((SLICES, 8, HD), f32),
-            dma((HK, 2)), dma((HK, 2)), dma((2,)), dma((1,)), dma((2,)), dma((2,)),
+            dma((HK, 2)), dma((HK, 2)), dma((HK,)), dma((1,)), dma((1,)), dma((2,)), dma((2,)),
             dma((HK + 1, N)), dma((HK + 1, N)), dma((HK,)),
             dma((HK, 2)), dma((HK, 2)),
             dma((SLICES,)), dma((8,)), dma((4,)), dma((4,)),

time: 78.4 us -> 77.4 us (0.987)
  Pallas kernels: 77.7 us -> 76.6 us
    pallas_call x1, Pallas kernels: 75 us -> 73.9 us  [local(): pl.pallas_call(kernel, out_shape=(jax.ShapeDtypeStruct((N, 2, BLK, (HQ +...]
where the time goes in v4:
time: 77.4 us; the launch traced here: 77.2 us
  Pallas kernels  76.6 us (99%)
    pallas_call x1, Pallas kernels, local(): pl.pallas_call(kernel, out_shape=(jax.ShapeDtypeStruct((N, 2, BLK, (HQ +...  73.9 us
    pallas_call x1, Pallas kernels, local(): pl.pallas_call(lay_out, out_shape=(shape((N, BLK, HQ * HD), bf16), shape(...  2.68 us

profile of v4, /device:TPU:1, one launch (start us, length us, event | category | flops | bytes accessed | tf_op | source)
XLA Modules:
  0.0 77.2 jit_solution(13149464342850048802)
XLA Ops:
  0.6 73.9 %shard_map.101 = (bf16[16,2,8,4608]{3,2,1,0:T(8,128)(2,1)}, f32[5,8,128]{2,1,0:T(8,128)}) custom-call(s32[1,16]{1,0:T(1,128)} %len_hbm.1, s32[1,16,16]{2,1,0:T(8,128)} %place_hbm.1, bf16[128,4096]{1,0:T(8,128)(2,1)} %bitcast.9, bf16[128,512]{1,0:T(8,128)(2,1)} %bitcast.13, bf16[128,512]{1,0:T(8,128)(2,1)} %bitcast.14, bf16[128,4096]{1,0:T(8,128)(2,1)} %bitcast.10), custom_call_target="tpu_custom_call" | custom-call | flops 2415919104 | bytes 6291456 | tf_op jit(solution)/shard_map/pallas_call | solution.py:613
  74.5 2.7 %shard_map.102 = (bf16[16,8,4096]{2,1,0:T(8,128)(2,1)}, bf16[16,8,4096]{2,1,0:T(8,128)(2,1)}, bf16[16,8,512]{2,1,0:T(8,128)(2,1)}, bf16[16,8,512]{2,1,0:T(8,128)(2,1)}, f32[5,8,128]{2,1,0:T(8,128)}) custom-call(bf16[16,2,8,4608]{3,2,1,0:T(8,128)(2,1)} %get-tuple-element.12.rows_ref, f32[5,8,128]{2,1,0:T(8,128)} %get-tuple-element.13.bias_ref), custom_call_target="tpu_custom_call" | custom-call | bytes 5242880 | tf_op jit(solution)/shard_map/pallas_call | solution.py:665

commit v5 on v4

--- a/solution.py
+++ b/solution.py
@@ -21,7 +21,7 @@
 SCALE = 1.0 / math.sqrt(HD)
 LOG2E = math.log2(math.e)
 SLICES = HK + 1
-FIRST_OWNER = 3
+FIRST_OWNER = 2
 HELD = 3
 KEEP = 4
 EARLY = 2 * HD
@@ -261,7 +261,7 @@
             {"ctx": half * 8 + s + FIRST_OWNER},
         )
 
-    is_owner = inner >= FIRST_OWNER
+    is_owner = (inner >= FIRST_OWNER) & (inner < FIRST_OWNER + SLICES)
     is_held = inner >= 2
 
     def group_step(g, carry):

time: 77.4 us -> 76.9 us (level)
  no operation moved by 1% of the time
where the time goes in v5:
time: 76.9 us; the launch traced here: 76.8 us
  Pallas kernels  76.1 us (99%)
    pallas_call x1, Pallas kernels, local(): pl.pallas_call(kernel, out_shape=(jax.ShapeDtypeStruct((N, 2, BLK, (HQ +...  73.5 us
    pallas_call x1, Pallas kernels, local(): pl.pallas_call(lay_out, out_shape=(shape((N, BLK, HQ * HD), bf16), shape(...  2.68 us

profile of v5, /device:TPU:1, one launch (start us, length us, event | category | flops | bytes accessed | tf_op | source)
XLA Modules:
  0.0 76.8 jit_solution(6809956320490257675)
XLA Ops:
  0.6 73.5 %shard_map.101 = (bf16[16,2,8,4608]{3,2,1,0:T(8,128)(2,1)}, f32[5,8,128]{2,1,0:T(8,128)}) custom-call(s32[1,16]{1,0:T(1,128)} %len_hbm.1, s32[1,16,16]{2,1,0:T(8,128)} %place_hbm.1, bf16[128,4096]{1,0:T(8,128)(2,1)} %bitcast.9, bf16[128,512]{1,0:T(8,128)(2,1)} %bitcast.13, bf16[128,512]{1,0:T(8,128)(2,1)} %bitcast.14, bf16[128,4096]{1,0:T(8,128)(2,1)} %bitcast.10), custom_call_target="tpu_custom_call" | custom-call | flops 2415919104 | bytes 6291456 | tf_op jit(solution)/shard_map/pallas_call | solution.py:613
  74.1 2.7 %shard_map.102 = (bf16[16,8,4096]{2,1,0:T(8,128)(2,1)}, bf16[16,8,4096]{2,1,0:T(8,128)(2,1)}, bf16[16,8,512]{2,1,0:T(8,128)(2,1)}, bf16[16,8,512]{2,1,0:T(8,128)(2,1)}, f32[5,8,128]{2,1,0:T(8,128)}) custom-call(bf16[16,2,8,4608]{3,2,1,0:T(8,128)(2,1)} %get-tuple-element.12.rows_ref, f32[5,8,128]{2,1,0:T(8,128)} %get-tuple-element.13.bias_ref), custom_call_target="tpu_custom_call" | custom-call | bytes 5242880 | tf_op jit(solution)/shard_map/pallas_call | solution.py:665

commit v6 on v5

--- a/solution.py
+++ b/solution.py
@@ -183,11 +183,6 @@
                 def _():
                     to_relay(g).start()
 
-        @pl.when(is_relay)
-        def _():
-            to_relay(1).wait_recv()
-            relayed().start()
-
     lane = lax.broadcasted_iota(jnp.int32, (1, ROWS), 1)
     pos = me * ROWS + lane
     first = jnp.zeros((1, ROWS), jnp.int32)
@@ -209,6 +204,11 @@
         == lax.broadcasted_iota(jnp.int32, (GROUP * ROWS, HD), 1),
         1.0, 0.0,
     ).astype(jnp.bfloat16)
+
+    @pl.when(is_relay)
+    def _():
+        to_relay(1).wait_recv()
+        relayed().start()
 
     def has_before(g, slot):
         return (me >= 2 - slot) & (jnp.logical_not(returns(slot)) | (g == HK - 1))

time: 76.9 us -> 77 us (level)
  no operation moved by 1% of the time
where the time goes in v6:
time: 77 us; the launch traced here: 76.8 us
  Pallas kernels  76.2 us (99%)
    pallas_call x1, Pallas kernels, local(): pl.pallas_call(kernel, out_shape=(jax.ShapeDtypeStruct((N, 2, BLK, (HQ +...  73.5 us
    pallas_call x1, Pallas kernels, local(): pl.pallas_call(lay_out, out_shape=(shape((N, BLK, HQ * HD), bf16), shape(...  2.68 us

profile of v6, /device:TPU:1, one launch (start us, length us, event | category | flops | bytes accessed | tf_op | source)
XLA Modules:
  0.0 76.8 jit_solution(13839866308700410692)
XLA Ops:
  0.6 73.5 %shard_map.101 = (bf16[16,2,8,4608]{3,2,1,0:T(8,128)(2,1)}, f32[5,8,128]{2,1,0:T(8,128)}) custom-call(s32[1,16]{1,0:T(1,128)} %len_hbm.1, s32[1,16,16]{2,1,0:T(8,128)} %place_hbm.1, bf16[128,4096]{1,0:T(8,128)(2,1)} %bitcast.9, bf16[128,512]{1,0:T(8,128)(2,1)} %bitcast.13, bf16[128,512]{1,0:T(8,128)(2,1)} %bitcast.14, bf16[128,4096]{1,0:T(8,128)(2,1)} %bitcast.10), custom_call_target="tpu_custom_call" | custom-call | flops 2415919104 | bytes 6291456 | tf_op jit(solution)/shard_map/pallas_call | solution.py:613
  74.1 2.7 %shard_map.102 = (bf16[16,8,4096]{2,1,0:T(8,128)(2,1)}, bf16[16,8,4096]{2,1,0:T(8,128)(2,1)}, bf16[16,8,512]{2,1,0:T(8,128)(2,1)}, bf16[16,8,512]{2,1,0:T(8,128)(2,1)}, f32[5,8,128]{2,1,0:T(8,128)}) custom-call(bf16[16,2,8,4608]{3,2,1,0:T(8,128)(2,1)} %get-tuple-element.12.rows_ref, f32[5,8,128]{2,1,0:T(8,128)} %get-tuple-element.13.bias_ref), custom_call_target="tpu_custom_call" | custom-call | bytes 5242880 | tf_op jit(solution)/shard_map/pallas_call | solution.py:665
